TPU v7x, 512 devices: a whole 4x4x16 slice. The times are simulated.
512 devices in a mesh: ctx: 16 (over z), kv: 8 (over y, x_lo), qh: 4 (over x_hi, core).
Axes of the slice: x: 4 (x_hi: 2, x_lo: 2; x = x_hi * 2 + x_lo), y: 4, z: 16, core: 2. Of those that a mesh axis runs over, the one named last changes fastest.
Arguments:
- queries: bfloat16 [8, 16, 384, 128], P('kv', 'qh', 'ctx'), may hold values from -16 to 16
- cache_keys: bfloat16 [8, 65536, 128], P('kv', 'ctx'), may hold values from -16 to 16
- cache_values: bfloat16 [8, 65536, 128], P('kv', 'ctx'), may hold values from -6 to 6
- cache_counts: int32 [16], P('ctx'), may hold values from 512 to 4096, as said below
- new_keys: bfloat16 [8, 384, 128], P('kv', ('ctx', 'qh')), may hold values from -16 to 16
- new_values: bfloat16 [8, 384, 128], P('kv', ('ctx', 'qh')), may hold values from -6 to 6
- new_positions: int32 [384], replicated, may hold values from 0 to 383, each once
Outputs:
- attended: bfloat16 [8, 16, 384, 128], P('kv', 'qh', 'ctx')
Inputs may be any that keep to these rules, and one draw needn't show every extreme that they name: `cache_counts`: one shard holds 4096 filled slots and another 4096 // 8. `new_positions`: each of 0 to 383 once; all cached tokens precede the new ones.
All inputs are finite; a program needn't handle non-finite values.
Results may differ from a plain program's by a relative error of at most 0.006.
Values may be sent and summed in bfloat16 or wider, within the bound.
A program may use at most 64 MiB of HBM per device.

v0:
```python
import jax
import jax.numpy as jnp
from jax import lax
from jax.sharding import PartitionSpec as P


def from_behind(block, axis, distance):
    devices = range(lax.axis_size(axis))
    route = [((i - distance) % len(devices), i) for i in devices]
    return lax.ppermute(block, axis, route)


def attend(query_rows, key_rows, value_rows, allowed):
    scores = lax.dot_general(
        query_rows, key_rows, (((1,), (1,)), ((), ())), preferred_element_type=jnp.float32
    ) * key_rows.shape[1] ** (-0.5)
    masked = jnp.where(allowed, scores, -jnp.inf)
    highest = jnp.max(masked, axis=1)
    weights = jnp.where(allowed, jnp.exp(scores - highest[:, None]), 0.0).astype(jnp.bfloat16)
    weighted = jnp.dot(weights, value_rows, preferred_element_type=jnp.float32)
    weight_sum = jnp.sum(weights.astype(jnp.float32), axis=1)
    return (highest, weighted, weight_sum)


def absorb(query_rows, numerator, denominator, highest, key_rows, value_rows, allowed):
    shard_peak, shard_sum, shard_mass = attend(query_rows, key_rows, value_rows, allowed)
    merged = jnp.maximum(highest, shard_peak)
    old_scale = jnp.exp(highest - merged)
    new_scale = jnp.exp(shard_peak - merged)
    numerator = numerator * old_scale[:, None] + shard_sum * new_scale[:, None]
    denominator = denominator * old_scale + shard_mass * new_scale
    return (numerator, denominator, merged)


def per_device(
    queries, cache_keys, cache_values, cache_counts, new_keys, new_values, new_positions
):
    head_count = queries.shape[1]
    row_count = queries.shape[2]
    head_width = queries.shape[3]
    key_rows = cache_keys[0]
    value_rows = cache_values[0]
    filled = cache_counts[0]
    slot_index = jnp.arange(key_rows.shape[0])
    valid_slots = (slot_index < filled)[None, :]
    fresh_keys, fresh_values = (
        lax.all_gather(new_keys, ("ctx", "qh"), axis=1, tiled=True),
        lax.all_gather(new_values, ("ctx", "qh"), axis=1, tiled=True),
    )
    offset = lax.axis_index("ctx") * row_count
    own_places = lax.dynamic_slice_in_dim(new_positions, offset, row_count)
    row_places = jnp.tile(own_places, head_count)
    causal = new_positions[None, :] <= row_places[:, None]
    query_rows = queries.reshape(head_count * row_count, head_width)
    fresh_peak, fresh_sum, fresh_mass = attend(query_rows, fresh_keys[0], fresh_values[0], causal)
    shard_total = lax.axis_size("ctx")

    def turn(turn_index, carried):
        visiting, numerator, denominator, highest = carried
        numerator, denominator, highest = absorb(
            visiting, numerator, denominator, highest, key_rows, value_rows, valid_slots
        )
        visiting = from_behind(visiting, "ctx", 1)
        numerator, denominator, highest = from_behind((numerator, denominator, highest), "ctx", 1)
        return (visiting, numerator, denominator, highest)

    finished = lax.fori_loop(0, shard_total, turn, (query_rows, fresh_sum, fresh_mass, fresh_peak))
    result = finished[1] / finished[2][:, None]
    return result.astype(jnp.bfloat16).reshape(queries.shape)


def solution(mesh):
    placed = (
        P("kv", "qh", "ctx", None),
        P("kv", "ctx", None),
        P("kv", "ctx", None),
        P("ctx"),
        P("kv", ("ctx", "qh"), None),
        P("kv", ("ctx", "qh"), None),
        P(),
    )
    return jax.shard_map(
        per_device,
        mesh=mesh,
        in_specs=placed,
        out_specs=P("kv", "qh", "ctx", None),
        check_vma=False,
    )
```

profile of v0, /device:TPU:24, one launch (start us, length us, event | category | flops | bytes accessed | tf_op | source)
XLA Modules:
  0.0 458.3 jit_solution(17707689437475532484)
XLA Ops:
  3.0 83.7 %all_gather.7 = bf16[1,384,128]{2,0,1:T(2,128)(2,1)S(1)} all-gather(bf16[1,6,128]{2,0,1:T(2,128)(2,1)S(1)} %copy.11), channel_id=1, replica_groups=mesh['ctx'=16,'kv'=8,'qh'=4] {'ctx','qh'}, dimensions={1}, use_global_device_ids=true | all-gather | bytes 99840 | tf_op jit(solution)/shard_map/all_gather | solution.py:48
  86.7 72.1 %all_gather.6 = bf16[1,384,128]{2,0,1:T(2,128)(2,1)S(1)} all-gather(bf16[1,6,128]{2,0,1:T(2,128)(2,1)S(1)} %copy.10), channel_id=1, replica_groups=mesh['ctx'=16,'kv'=8,'qh'=4] {'ctx','qh'}, dimensions={1}, use_global_device_ids=true | all-gather | bytes 99840 | tf_op jit(solution)/shard_map/all_gather | solution.py:47
  160.8 296.8 %while.17 = (s32[]{:T(128)}, bf16[96,128]{1,0:T(8,128)(2,1)S(1)}, f32[96,128]{1,0:T(8,128)S(1)}, f32[96]{0:T(128)S(1)}, f32[96]{0:T(128)S(1)}, /*index=5*/bf16[4...) while((s32[]{:T(128)}, bf16[96,128]{1,0:T(8,128)(2,1)S(1)}, ...), condition=%wide.region_5.6_spmd.clone, body=%wide.region_2.5_spmd.clone.sunk | while | flops 205693312 | bytes 11502109 | solution.py:67
  170.2 2.0 collective-permute-start.3
  172.1 2.7 collective-permute-done.2
  184.2 3.6 collective-permute-start.2
  187.9 5.7 %collective-permute-start.3 = (f32[96]{0:T(128)S(1)}, f32[96]{0:T(128)S(1)}, u32[]{:S(2)}, u32[]{:S(2)}) collective-permute-start(f32[96]{0:T(128)S(1)} %get-tuple-element.155), channel_id=1, source_target_pairs={{480,0},{0,32},{32,64},{64,96},{96,128},{128,160},{160,192},{192,2... | collective-permute-start | bytes 1160 | tf_op jit(solution)/shard_map/while/body/eval_jaxpr/ppermute | solution.py:10
  198.4 4.2 collective-permute-start.1
  202.5 4.2 collective-permute-start
  208.6 3.1 collective-permute-start.3
  218.8 1.9 collective-permute-start.1
  220.8 4.0 collective-permute-start
  224.8 4.2 collective-permute-start.2
  228.9 3.1 collective-permute-start.3
  232.1 3.5 collective-permute-done.3
  243.0 2.5 collective-permute-start.2
  245.5 5.4 %collective-permute-start.3 = (f32[96]{0:T(128)S(1)}, f32[96]{0:T(128)S(1)}, u32[]{:S(2)}, u32[]{:S(2)}) collective-permute-start(f32[96]{0:T(128)S(1)} %get-tuple-element.155), channel_id=1, source_target_pairs={{480,0},{0,32},{32,64},{64,96},{96,128},{128,160},{160,192},{192,2... | collective-permute-start | bytes 1160 | tf_op jit(solution)/shard_map/while/body/eval_jaxpr/ppermute | solution.py:10
  255.8 4.2 collective-permute-start.1
  263.8 3.1 collective-permute-start.3
  279.8 5.1 %collective-permute-start.3 = (f32[96]{0:T(128)S(1)}, f32[96]{0:T(128)S(1)}, u32[]{:S(2)}, u32[]{:S(2)}) collective-permute-start(f32[96]{0:T(128)S(1)} %get-tuple-element.155), channel_id=1, source_target_pairs={{480,0},{0,32},{32,64},{64,96},{96,128},{128,160},{160,192},{192,2... | collective-permute-start | bytes 1160 | tf_op jit(solution)/shard_map/while/body/eval_jaxpr/ppermute | solution.py:10
  290.0 3.9 collective-permute-start.1
  293.9 4.2 collective-permute-start
  298.1 4.2 collective-permute-start.2
  302.2 3.1 collective-permute-start.3
  305.4 3.5 collective-permute-done.3
  314.4 1.9 collective-permute-start
  316.3 4.0 collective-permute-start.2
  320.3 5.4 %collective-permute-start.3 = (f32[96]{0:T(128)S(1)}, f32[96]{0:T(128)S(1)}, u32[]{:S(2)}, u32[]{:S(2)}) collective-permute-start(f32[96]{0:T(128)S(1)} %get-tuple-element.155), channel_id=1, source_target_pairs={{480,0},{0,32},{32,64},{64,96},{96,128},{128,160},{160,192},{192,2... | collective-permute-start | bytes 1160 | tf_op jit(solution)/shard_map/while/body/eval_jaxpr/ppermute | solution.py:10
  330.5 4.2 collective-permute-start.1
  338.5 3.7 collective-permute-start.3
  348.8 2.5 collective-permute-start.1
  351.3 4.2 collective-permute-start
  357.4 3.1 collective-permute-start.3
  369.5 1.9 collective-permute-start
  373.4 3.1 collective-permute-start.3
  385.6 3.9 collective-permute-start
  389.5 4.2 collective-permute-start.2
  393.6 5.4 %collective-permute-start.3 = (f32[96]{0:T(128)S(1)}, f32[96]{0:T(128)S(1)}, u32[]{:S(2)}, u32[]{:S(2)}) collective-permute-start(f32[96]{0:T(128)S(1)} %get-tuple-element.155), channel_id=1, source_target_pairs={{480,0},{0,32},{32,64},{64,96},{96,128},{128,160},{160,192},{192,2... | collective-permute-start | bytes 1160 | tf_op jit(solution)/shard_map/while/body/eval_jaxpr/ppermute | solution.py:10
  403.8 4.2 collective-permute-start.1
  409.9 1.9 collective-permute-start.2
  411.9 5.2 %collective-permute-start.3 = (f32[96]{0:T(128)S(1)}, f32[96]{0:T(128)S(1)}, u32[]{:S(2)}, u32[]{:S(2)}) collective-permute-start(f32[96]{0:T(128)S(1)} %get-tuple-element.155), channel_id=1, source_target_pairs={{480,0},{0,32},{32,64},{64,96},{96,128},{128,160},{160,192},{192,2... | collective-permute-start | bytes 1160 | tf_op jit(solution)/shard_map/while/body/eval_jaxpr/ppermute | solution.py:10
  422.1 4.0 collective-permute-start.1
  426.1 4.2 collective-permute-start
  432.2 3.1 collective-permute-start.3
  444.3 2.5 collective-permute-start
  446.8 4.2 collective-permute-start.2
  451.0 3.1 collective-permute-start.3
  454.1 3.5 collective-permute-done.3
  (221 shorter events, 136.7 us)
Async XLA Ops:
  164.4 12.4 %collective-permute-start.1 = (f32[96,128]{1,0:T(8,128)S(1)}, f32[96,128]{1,0:T(8,128)S(1)}, u32[]{:S(2)}, u32[]{:S(2)}) collective-permute-start(f32[96,128]{1,0:T(8,128)S(1)} %fusion.23), channel_id=1, source_target_pairs={{480,0},{0,32},{32,64},{64,96},{96,128},{128,160},{160,192},{192,2... | collective-permute-start | bytes 147464 | tf_op jit(solution)/shard_map/while/body/eval_jaxpr/ppermute | solution.py:10
  166.3 10.5 %collective-permute-start = (bf16[96,128]{1,0:T(8,128)(2,1)S(1)}, bf16[96,128]{1,0:T(8,128)(2,1)S(1)}, u32[]{:S(2)}, u32[]{:S(2)}) collective-permute-start(bf16[96,128]{1,0:T(8,128)(2,1)S(1)} %copy.30), channel_id=1, source_target_pairs={{480,0},{0,32},{32,64},{64,96},{96,128},{128,160},{160,192},{192,2... | collective-permute-start | bytes 73736 | tf_op jit(solution)/shard_map/while/body/eval_jaxpr/ppermute | solution.py:10
  180.4 14.4 %collective-permute-start.1 = (f32[96,128]{1,0:T(8,128)S(1)}, f32[96,128]{1,0:T(8,128)S(1)}, u32[]{:S(2)}, u32[]{:S(2)}) collective-permute-start(f32[96,128]{1,0:T(8,128)S(1)} %fusion.23), channel_id=1, source_target_pairs={{480,0},{0,32},{32,64},{64,96},{96,128},{128,160},{160,192},{192,2... | collective-permute-start | bytes 147464 | tf_op jit(solution)/shard_map/while/body/eval_jaxpr/ppermute | solution.py:10
  182.3 12.5 %collective-permute-start = (bf16[96,128]{1,0:T(8,128)(2,1)S(1)}, bf16[96,128]{1,0:T(8,128)(2,1)S(1)}, u32[]{:S(2)}, u32[]{:S(2)}) collective-permute-start(bf16[96,128]{1,0:T(8,128)(2,1)S(1)} %copy.30), channel_id=1, source_target_pairs={{480,0},{0,32},{32,64},{64,96},{96,128},{128,160},{160,192},{192,2... | collective-permute-start | bytes 73736 | tf_op jit(solution)/shard_map/while/body/eval_jaxpr/ppermute | solution.py:10
  184.2 9.3 %collective-permute-start.2 = (f32[96]{0:T(128)S(1)}, f32[96]{0:T(128)S(1)}, u32[]{:S(2)}, u32[]{:S(2)}) collective-permute-start(f32[96]{0:T(128)S(1)} %get-tuple-element.154), channel_id=1, source_target_pairs={{480,0},{0,32},{32,64},{64,96},{96,128},{128,160},{160,192},{192,2... | collective-permute-start | bytes 1160 | tf_op jit(solution)/shard_map/while/body/eval_jaxpr/ppermute | solution.py:10
  187.9 6.9 %collective-permute-start.3 = (f32[96]{0:T(128)S(1)}, f32[96]{0:T(128)S(1)}, u32[]{:S(2)}, u32[]{:S(2)}) collective-permute-start(f32[96]{0:T(128)S(1)} %get-tuple-element.155), channel_id=1, source_target_pairs={{480,0},{0,32},{32,64},{64,96},{96,128},{128,160},{160,192},{192,2... | collective-permute-start | bytes 1160 | tf_op jit(solution)/shard_map/while/body/eval_jaxpr/ppermute | solution.py:10
  198.4 16.9 %collective-permute-start.1 = (f32[96,128]{1,0:T(8,128)S(1)}, f32[96,128]{1,0:T(8,128)S(1)}, u32[]{:S(2)}, u32[]{:S(2)}) collective-permute-start(f32[96,128]{1,0:T(8,128)S(1)} %fusion.23), channel_id=1, source_target_pairs={{480,0},{0,32},{32,64},{64,96},{96,128},{128,160},{160,192},{192,2... | collective-permute-start | bytes 147464 | tf_op jit(solution)/shard_map/while/body/eval_jaxpr/ppermute | solution.py:10
  202.5 12.7 %collective-permute-start = (bf16[96,128]{1,0:T(8,128)(2,1)S(1)}, bf16[96,128]{1,0:T(8,128)(2,1)S(1)}, u32[]{:S(2)}, u32[]{:S(2)}) collective-permute-start(bf16[96,128]{1,0:T(8,128)(2,1)S(1)} %copy.30), channel_id=1, source_target_pairs={{480,0},{0,32},{32,64},{64,96},{96,128},{128,160},{160,192},{192,2... | collective-permute-start | bytes 73736 | tf_op jit(solution)/shard_map/while/body/eval_jaxpr/ppermute | solution.py:10
  206.7 6.6 %collective-permute-start.2 = (f32[96]{0:T(128)S(1)}, f32[96]{0:T(128)S(1)}, u32[]{:S(2)}, u32[]{:S(2)}) collective-permute-start(f32[96]{0:T(128)S(1)} %get-tuple-element.154), channel_id=1, source_target_pairs={{480,0},{0,32},{32,64},{64,96},{96,128},{128,160},{160,192},{192,2... | collective-permute-start | bytes 1160 | tf_op jit(solution)/shard_map/while/body/eval_jaxpr/ppermute | solution.py:10
  208.6 6.6 %collective-permute-start.3 = (f32[96]{0:T(128)S(1)}, f32[96]{0:T(128)S(1)}, u32[]{:S(2)}, u32[]{:S(2)}) collective-permute-start(f32[96]{0:T(128)S(1)} %get-tuple-element.155), channel_id=1, source_target_pairs={{480,0},{0,32},{32,64},{64,96},{96,128},{128,160},{160,192},{192,2... | collective-permute-start | bytes 1160 | tf_op jit(solution)/shard_map/while/body/eval_jaxpr/ppermute | solution.py:10
  218.8 16.7 %collective-permute-start.1 = (f32[96,128]{1,0:T(8,128)S(1)}, f32[96,128]{1,0:T(8,128)S(1)}, u32[]{:S(2)}, u32[]{:S(2)}) collective-permute-start(f32[96,128]{1,0:T(8,128)S(1)} %fusion.23), channel_id=1, source_target_pairs={{480,0},{0,32},{32,64},{64,96},{96,128},{128,160},{160,192},{192,2... | collective-permute-start | bytes 147464 | tf_op jit(solution)/shard_map/while/body/eval_jaxpr/ppermute | solution.py:10
  220.8 14.8 %collective-permute-start = (bf16[96,128]{1,0:T(8,128)(2,1)S(1)}, bf16[96,128]{1,0:T(8,128)(2,1)S(1)}, u32[]{:S(2)}, u32[]{:S(2)}) collective-permute-start(bf16[96,128]{1,0:T(8,128)(2,1)S(1)} %copy.30), channel_id=1, source_target_pairs={{480,0},{0,32},{32,64},{64,96},{96,128},{128,160},{160,192},{192,2... | collective-permute-start | bytes 73736 | tf_op jit(solution)/shard_map/while/body/eval_jaxpr/ppermute | solution.py:10
  224.8 7.3 %collective-permute-start.2 = (f32[96]{0:T(128)S(1)}, f32[96]{0:T(128)S(1)}, u32[]{:S(2)}, u32[]{:S(2)}) collective-permute-start(f32[96]{0:T(128)S(1)} %get-tuple-element.154), channel_id=1, source_target_pairs={{480,0},{0,32},{32,64},{64,96},{96,128},{128,160},{160,192},{192,2... | collective-permute-start | bytes 1160 | tf_op jit(solution)/shard_map/while/body/eval_jaxpr/ppermute | solution.py:10
  228.9 6.6 %collective-permute-start.3 = (f32[96]{0:T(128)S(1)}, f32[96]{0:T(128)S(1)}, u32[]{:S(2)}, u32[]{:S(2)}) collective-permute-start(f32[96]{0:T(128)S(1)} %get-tuple-element.155), channel_id=1, source_target_pairs={{480,0},{0,32},{32,64},{64,96},{96,128},{128,160},{160,192},{192,2... | collective-permute-start | bytes 1160 | tf_op jit(solution)/shard_map/while/body/eval_jaxpr/ppermute | solution.py:10
  239.2 13.0 %collective-permute-start.1 = (f32[96,128]{1,0:T(8,128)S(1)}, f32[96,128]{1,0:T(8,128)S(1)}, u32[]{:S(2)}, u32[]{:S(2)}) collective-permute-start(f32[96,128]{1,0:T(8,128)S(1)} %fusion.23), channel_id=1, source_target_pairs={{480,0},{0,32},{32,64},{64,96},{96,128},{128,160},{160,192},{192,2... | collective-permute-start | bytes 147464 | tf_op jit(solution)/shard_map/while/body/eval_jaxpr/ppermute | solution.py:10
  241.1 11.1 %collective-permute-start = (bf16[96,128]{1,0:T(8,128)(2,1)S(1)}, bf16[96,128]{1,0:T(8,128)(2,1)S(1)}, u32[]{:S(2)}, u32[]{:S(2)}) collective-permute-start(bf16[96,128]{1,0:T(8,128)(2,1)S(1)} %copy.30), channel_id=1, source_target_pairs={{480,0},{0,32},{32,64},{64,96},{96,128},{128,160},{160,192},{192,2... | collective-permute-start | bytes 73736 | tf_op jit(solution)/shard_map/while/body/eval_jaxpr/ppermute | solution.py:10
  243.0 7.9 %collective-permute-start.2 = (f32[96]{0:T(128)S(1)}, f32[96]{0:T(128)S(1)}, u32[]{:S(2)}, u32[]{:S(2)}) collective-permute-start(f32[96]{0:T(128)S(1)} %get-tuple-element.154), channel_id=1, source_target_pairs={{480,0},{0,32},{32,64},{64,96},{96,128},{128,160},{160,192},{192,2... | collective-permute-start | bytes 1160 | tf_op jit(solution)/shard_map/while/body/eval_jaxpr/ppermute | solution.py:10
  245.5 6.6 %collective-permute-start.3 = (f32[96]{0:T(128)S(1)}, f32[96]{0:T(128)S(1)}, u32[]{:S(2)}, u32[]{:S(2)}) collective-permute-start(f32[96]{0:T(128)S(1)} %get-tuple-element.155), channel_id=1, source_target_pairs={{480,0},{0,32},{32,64},{64,96},{96,128},{128,160},{160,192},{192,2... | collective-permute-start | bytes 1160 | tf_op jit(solution)/shard_map/while/body/eval_jaxpr/ppermute | solution.py:10
  255.8 14.7 %collective-permute-start.1 = (f32[96,128]{1,0:T(8,128)S(1)}, f32[96,128]{1,0:T(8,128)S(1)}, u32[]{:S(2)}, u32[]{:S(2)}) collective-permute-start(f32[96,128]{1,0:T(8,128)S(1)} %fusion.23), channel_id=1, source_target_pairs={{480,0},{0,32},{32,64},{64,96},{96,128},{128,160},{160,192},{192,2... | collective-permute-start | bytes 147464 | tf_op jit(solution)/shard_map/while/body/eval_jaxpr/ppermute | solution.py:10
  259.9 10.5 %collective-permute-start = (bf16[96,128]{1,0:T(8,128)(2,1)S(1)}, bf16[96,128]{1,0:T(8,128)(2,1)S(1)}, u32[]{:S(2)}, u32[]{:S(2)}) collective-permute-start(bf16[96,128]{1,0:T(8,128)(2,1)S(1)} %copy.30), channel_id=1, source_target_pairs={{480,0},{0,32},{32,64},{64,96},{96,128},{128,160},{160,192},{192,2... | collective-permute-start | bytes 73736 | tf_op jit(solution)/shard_map/while/body/eval_jaxpr/ppermute | solution.py:10
  263.8 6.6 %collective-permute-start.3 = (f32[96]{0:T(128)S(1)}, f32[96]{0:T(128)S(1)}, u32[]{:S(2)}, u32[]{:S(2)}) collective-permute-start(f32[96]{0:T(128)S(1)} %get-tuple-element.155), channel_id=1, source_target_pairs={{480,0},{0,32},{32,64},{64,96},{96,128},{128,160},{160,192},{192,2... | collective-permute-start | bytes 1160 | tf_op jit(solution)/shard_map/while/body/eval_jaxpr/ppermute | solution.py:10
  274.0 12.4 %collective-permute-start.1 = (f32[96,128]{1,0:T(8,128)S(1)}, f32[96,128]{1,0:T(8,128)S(1)}, u32[]{:S(2)}, u32[]{:S(2)}) collective-permute-start(f32[96,128]{1,0:T(8,128)S(1)} %fusion.23), channel_id=1, source_target_pairs={{480,0},{0,32},{32,64},{64,96},{96,128},{128,160},{160,192},{192,2... | collective-permute-start | bytes 147464 | tf_op jit(solution)/shard_map/while/body/eval_jaxpr/ppermute | solution.py:10
  275.9 10.5 %collective-permute-start = (bf16[96,128]{1,0:T(8,128)(2,1)S(1)}, bf16[96,128]{1,0:T(8,128)(2,1)S(1)}, u32[]{:S(2)}, u32[]{:S(2)}) collective-permute-start(bf16[96,128]{1,0:T(8,128)(2,1)S(1)} %copy.30), channel_id=1, source_target_pairs={{480,0},{0,32},{32,64},{64,96},{96,128},{128,160},{160,192},{192,2... | collective-permute-start | bytes 73736 | tf_op jit(solution)/shard_map/while/body/eval_jaxpr/ppermute | solution.py:10
  277.9 7.1 %collective-permute-start.2 = (f32[96]{0:T(128)S(1)}, f32[96]{0:T(128)S(1)}, u32[]{:S(2)}, u32[]{:S(2)}) collective-permute-start(f32[96]{0:T(128)S(1)} %get-tuple-element.154), channel_id=1, source_target_pairs={{480,0},{0,32},{32,64},{64,96},{96,128},{128,160},{160,192},{192,2... | collective-permute-start | bytes 1160 | tf_op jit(solution)/shard_map/while/body/eval_jaxpr/ppermute | solution.py:10
  279.8 6.6 %collective-permute-start.3 = (f32[96]{0:T(128)S(1)}, f32[96]{0:T(128)S(1)}, u32[]{:S(2)}, u32[]{:S(2)}) collective-permute-start(f32[96]{0:T(128)S(1)} %get-tuple-element.155), channel_id=1, source_target_pairs={{480,0},{0,32},{32,64},{64,96},{96,128},{128,160},{160,192},{192,2... | collective-permute-start | bytes 1160 | tf_op jit(solution)/shard_map/while/body/eval_jaxpr/ppermute | solution.py:10
  290.0 18.9 %collective-permute-start.1 = (f32[96,128]{1,0:T(8,128)S(1)}, f32[96,128]{1,0:T(8,128)S(1)}, u32[]{:S(2)}, u32[]{:S(2)}) collective-permute-start(f32[96,128]{1,0:T(8,128)S(1)} %fusion.23), channel_id=1, source_target_pairs={{480,0},{0,32},{32,64},{64,96},{96,128},{128,160},{160,192},{192,2... | collective-permute-start | bytes 147464 | tf_op jit(solution)/shard_map/while/body/eval_jaxpr/ppermute | solution.py:10
  293.9 15.0 %collective-permute-start = (bf16[96,128]{1,0:T(8,128)(2,1)S(1)}, bf16[96,128]{1,0:T(8,128)(2,1)S(1)}, u32[]{:S(2)}, u32[]{:S(2)}) collective-permute-start(bf16[96,128]{1,0:T(8,128)(2,1)S(1)} %copy.30), channel_id=1, source_target_pairs={{480,0},{0,32},{32,64},{64,96},{96,128},{128,160},{160,192},{192,2... | collective-permute-start | bytes 73736 | tf_op jit(solution)/shard_map/while/body/eval_jaxpr/ppermute | solution.py:10
  298.1 7.3 %collective-permute-start.2 = (f32[96]{0:T(128)S(1)}, f32[96]{0:T(128)S(1)}, u32[]{:S(2)}, u32[]{:S(2)}) collective-permute-start(f32[96]{0:T(128)S(1)} %get-tuple-element.154), channel_id=1, source_target_pairs={{480,0},{0,32},{32,64},{64,96},{96,128},{128,160},{160,192},{192,2... | collective-permute-start | bytes 1160 | tf_op jit(solution)/shard_map/while/body/eval_jaxpr/ppermute | solution.py:10
  312.5 14.5 %collective-permute-start.1 = (f32[96,128]{1,0:T(8,128)S(1)}, f32[96,128]{1,0:T(8,128)S(1)}, u32[]{:S(2)}, u32[]{:S(2)}) collective-permute-start(f32[96,128]{1,0:T(8,128)S(1)} %fusion.23), channel_id=1, source_target_pairs={{480,0},{0,32},{32,64},{64,96},{96,128},{128,160},{160,192},{192,2... | collective-permute-start | bytes 147464 | tf_op jit(solution)/shard_map/while/body/eval_jaxpr/ppermute | solution.py:10
  314.4 12.6 %collective-permute-start = (bf16[96,128]{1,0:T(8,128)(2,1)S(1)}, bf16[96,128]{1,0:T(8,128)(2,1)S(1)}, u32[]{:S(2)}, u32[]{:S(2)}) collective-permute-start(bf16[96,128]{1,0:T(8,128)(2,1)S(1)} %copy.30), channel_id=1, source_target_pairs={{480,0},{0,32},{32,64},{64,96},{96,128},{128,160},{160,192},{192,2... | collective-permute-start | bytes 73736 | tf_op jit(solution)/shard_map/while/body/eval_jaxpr/ppermute | solution.py:10
  316.3 9.4 %collective-permute-start.2 = (f32[96]{0:T(128)S(1)}, f32[96]{0:T(128)S(1)}, u32[]{:S(2)}, u32[]{:S(2)}) collective-permute-start(f32[96]{0:T(128)S(1)} %get-tuple-element.154), channel_id=1, source_target_pairs={{480,0},{0,32},{32,64},{64,96},{96,128},{128,160},{160,192},{192,2... | collective-permute-start | bytes 1160 | tf_op jit(solution)/shard_map/while/body/eval_jaxpr/ppermute | solution.py:10
  330.5 14.7 %collective-permute-start.1 = (f32[96,128]{1,0:T(8,128)S(1)}, f32[96,128]{1,0:T(8,128)S(1)}, u32[]{:S(2)}, u32[]{:S(2)}) collective-permute-start(f32[96,128]{1,0:T(8,128)S(1)} %fusion.23), channel_id=1, source_target_pairs={{480,0},{0,32},{32,64},{64,96},{96,128},{128,160},{160,192},{192,2... | collective-permute-start | bytes 147464 | tf_op jit(solution)/shard_map/while/body/eval_jaxpr/ppermute | solution.py:10
  334.7 10.5 %collective-permute-start = (bf16[96,128]{1,0:T(8,128)(2,1)S(1)}, bf16[96,128]{1,0:T(8,128)(2,1)S(1)}, u32[]{:S(2)}, u32[]{:S(2)}) collective-permute-start(bf16[96,128]{1,0:T(8,128)(2,1)S(1)} %copy.30), channel_id=1, source_target_pairs={{480,0},{0,32},{32,64},{64,96},{96,128},{128,160},{160,192},{192,2... | collective-permute-start | bytes 73736 | tf_op jit(solution)/shard_map/while/body/eval_jaxpr/ppermute | solution.py:10
  348.8 15.3 %collective-permute-start.1 = (f32[96,128]{1,0:T(8,128)S(1)}, f32[96,128]{1,0:T(8,128)S(1)}, u32[]{:S(2)}, u32[]{:S(2)}) collective-permute-start(f32[96,128]{1,0:T(8,128)S(1)} %fusion.23), channel_id=1, source_target_pairs={{480,0},{0,32},{32,64},{64,96},{96,128},{128,160},{160,192},{192,2... | collective-permute-start | bytes 147464 | tf_op jit(solution)/shard_map/while/body/eval_jaxpr/ppermute | solution.py:10
  351.3 12.7 %collective-permute-start = (bf16[96,128]{1,0:T(8,128)(2,1)S(1)}, bf16[96,128]{1,0:T(8,128)(2,1)S(1)}, u32[]{:S(2)}, u32[]{:S(2)}) collective-permute-start(bf16[96,128]{1,0:T(8,128)(2,1)S(1)} %copy.30), channel_id=1, source_target_pairs={{480,0},{0,32},{32,64},{64,96},{96,128},{128,160},{160,192},{192,2... | collective-permute-start | bytes 73736 | tf_op jit(solution)/shard_map/while/body/eval_jaxpr/ppermute | solution.py:10
  367.6 12.5 %collective-permute-start.1 = (f32[96,128]{1,0:T(8,128)S(1)}, f32[96,128]{1,0:T(8,128)S(1)}, u32[]{:S(2)}, u32[]{:S(2)}) collective-permute-start(f32[96,128]{1,0:T(8,128)S(1)} %fusion.23), channel_id=1, source_target_pairs={{480,0},{0,32},{32,64},{64,96},{96,128},{128,160},{160,192},{192,2... | collective-permute-start | bytes 147464 | tf_op jit(solution)/shard_map/while/body/eval_jaxpr/ppermute | solution.py:10
  369.5 10.5 %collective-permute-start = (bf16[96,128]{1,0:T(8,128)(2,1)S(1)}, bf16[96,128]{1,0:T(8,128)(2,1)S(1)}, u32[]{:S(2)}, u32[]{:S(2)}) collective-permute-start(bf16[96,128]{1,0:T(8,128)(2,1)S(1)} %copy.30), channel_id=1, source_target_pairs={{480,0},{0,32},{32,64},{64,96},{96,128},{128,160},{160,192},{192,2... | collective-permute-start | bytes 73736 | tf_op jit(solution)/shard_map/while/body/eval_jaxpr/ppermute | solution.py:10
  383.6 16.6 %collective-permute-start.1 = (f32[96,128]{1,0:T(8,128)S(1)}, f32[96,128]{1,0:T(8,128)S(1)}, u32[]{:S(2)}, u32[]{:S(2)}) collective-permute-start(f32[96,128]{1,0:T(8,128)S(1)} %fusion.23), channel_id=1, source_target_pairs={{480,0},{0,32},{32,64},{64,96},{96,128},{128,160},{160,192},{192,2... | collective-permute-start | bytes 147464 | tf_op jit(solution)/shard_map/while/body/eval_jaxpr/ppermute | solution.py:10
  385.6 14.7 %collective-permute-start = (bf16[96,128]{1,0:T(8,128)(2,1)S(1)}, bf16[96,128]{1,0:T(8,128)(2,1)S(1)}, u32[]{:S(2)}, u32[]{:S(2)}) collective-permute-start(bf16[96,128]{1,0:T(8,128)(2,1)S(1)} %copy.30), channel_id=1, source_target_pairs={{480,0},{0,32},{32,64},{64,96},{96,128},{128,160},{160,192},{192,2... | collective-permute-start | bytes 73736 | tf_op jit(solution)/shard_map/while/body/eval_jaxpr/ppermute | solution.py:10
  389.5 9.5 %collective-permute-start.2 = (f32[96]{0:T(128)S(1)}, f32[96]{0:T(128)S(1)}, u32[]{:S(2)}, u32[]{:S(2)}) collective-permute-start(f32[96]{0:T(128)S(1)} %get-tuple-element.154), channel_id=1, source_target_pairs={{480,0},{0,32},{32,64},{64,96},{96,128},{128,160},{160,192},{192,2... | collective-permute-start | bytes 1160 | tf_op jit(solution)/shard_map/while/body/eval_jaxpr/ppermute | solution.py:10
  403.8 14.7 %collective-permute-start.1 = (f32[96,128]{1,0:T(8,128)S(1)}, f32[96,128]{1,0:T(8,128)S(1)}, u32[]{:S(2)}, u32[]{:S(2)}) collective-permute-start(f32[96,128]{1,0:T(8,128)S(1)} %fusion.23), channel_id=1, source_target_pairs={{480,0},{0,32},{32,64},{64,96},{96,128},{128,160},{160,192},{192,2... | collective-permute-start | bytes 147464 | tf_op jit(solution)/shard_map/while/body/eval_jaxpr/ppermute | solution.py:10
  408.0 10.5 %collective-permute-start = (bf16[96,128]{1,0:T(8,128)(2,1)S(1)}, bf16[96,128]{1,0:T(8,128)(2,1)S(1)}, u32[]{:S(2)}, u32[]{:S(2)}) collective-permute-start(bf16[96,128]{1,0:T(8,128)(2,1)S(1)} %copy.30), channel_id=1, source_target_pairs={{480,0},{0,32},{32,64},{64,96},{96,128},{128,160},{160,192},{192,2... | collective-permute-start | bytes 73736 | tf_op jit(solution)/shard_map/while/body/eval_jaxpr/ppermute | solution.py:10
  409.9 7.1 %collective-permute-start.2 = (f32[96]{0:T(128)S(1)}, f32[96]{0:T(128)S(1)}, u32[]{:S(2)}, u32[]{:S(2)}) collective-permute-start(f32[96]{0:T(128)S(1)} %get-tuple-element.154), channel_id=1, source_target_pairs={{480,0},{0,32},{32,64},{64,96},{96,128},{128,160},{160,192},{192,2... | collective-permute-start | bytes 1160 | tf_op jit(solution)/shard_map/while/body/eval_jaxpr/ppermute | solution.py:10
  422.1 16.7 %collective-permute-start.1 = (f32[96,128]{1,0:T(8,128)S(1)}, f32[96,128]{1,0:T(8,128)S(1)}, u32[]{:S(2)}, u32[]{:S(2)}) collective-permute-start(f32[96,128]{1,0:T(8,128)S(1)} %fusion.23), channel_id=1, source_target_pairs={{480,0},{0,32},{32,64},{64,96},{96,128},{128,160},{160,192},{192,2... | collective-permute-start | bytes 147464 | tf_op jit(solution)/shard_map/while/body/eval_jaxpr/ppermute | solution.py:10
  426.1 12.7 %collective-permute-start = (bf16[96,128]{1,0:T(8,128)(2,1)S(1)}, bf16[96,128]{1,0:T(8,128)(2,1)S(1)}, u32[]{:S(2)}, u32[]{:S(2)}) collective-permute-start(bf16[96,128]{1,0:T(8,128)(2,1)S(1)} %copy.30), channel_id=1, source_target_pairs={{480,0},{0,32},{32,64},{64,96},{96,128},{128,160},{160,192},{192,2... | collective-permute-start | bytes 73736 | tf_op jit(solution)/shard_map/while/body/eval_jaxpr/ppermute | solution.py:10
  442.4 15.3 %collective-permute-start.1 = (f32[96,128]{1,0:T(8,128)S(1)}, f32[96,128]{1,0:T(8,128)S(1)}, u32[]{:S(2)}, u32[]{:S(2)}) collective-permute-start(f32[96,128]{1,0:T(8,128)S(1)} %fusion.23), channel_id=1, source_target_pairs={{480,0},{0,32},{32,64},{64,96},{96,128},{128,160},{160,192},{192,2... | collective-permute-start | bytes 147464 | tf_op jit(solution)/shard_map/while/body/eval_jaxpr/ppermute | solution.py:10
  444.3 13.3 %collective-permute-start = (bf16[96,128]{1,0:T(8,128)(2,1)S(1)}, bf16[96,128]{1,0:T(8,128)(2,1)S(1)}, u32[]{:S(2)}, u32[]{:S(2)}) collective-permute-start(bf16[96,128]{1,0:T(8,128)(2,1)S(1)} %copy.30), channel_id=1, source_target_pairs={{480,0},{0,32},{32,64},{64,96},{96,128},{128,160},{160,192},{192,2... | collective-permute-start | bytes 73736 | tf_op jit(solution)/shard_map/while/body/eval_jaxpr/ppermute | solution.py:10
  446.8 7.3 %collective-permute-start.2 = (f32[96]{0:T(128)S(1)}, f32[96]{0:T(128)S(1)}, u32[]{:S(2)}, u32[]{:S(2)}) collective-permute-start(f32[96]{0:T(128)S(1)} %get-tuple-element.154), channel_id=1, source_target_pairs={{480,0},{0,32},{32,64},{64,96},{96,128},{128,160},{160,192},{192,2... | collective-permute-start | bytes 1160 | tf_op jit(solution)/shard_map/while/body/eval_jaxpr/ppermute | solution.py:10
  (32 other events, 144.4 us)
where the time goes:
time: 461 us; the launch traced here: 458 us
  starting transfers between devices  195 us (42%)
  blocking collectives  156 us (34%)
  waiting for transfers between devices  43.6 us (9%)
  matrix products  38.6 us (8%)
  other arithmetic  20.4 us (4%)
    ppermute x64, starting transfers between devices, from_behind(): return lax.ppermute(block, axis, route)  195 us
    all_gather x1, blocking collectives, per_device(): lax.all_gather(new_values, ('ctx', 'qh'), axis=1, tiled=True)  83.7 us
    all_gather x1, blocking collectives, per_device(): lax.all_gather(new_keys, ('ctx', 'qh'), axis=1, tiled=True)  72.1 us
    ppermute x64, waiting for transfers between devices, from_behind(): return lax.ppermute(block, axis, route)  43.6 us
    dot_general x17, matrix products, attend(): lax.dot_general(query_rows, key_rows, (((1,), (1,)), ((), ())), preferred...  31.2 us
    lt x16, other arithmetic, per_device(): valid_slots = (slot_index < filled)[None, :]  11.3 us
  transfers between devices with their start and end apart: 64, of which 23 were waited for; matrix products, arithmetic and copies ran while one was open for 0% of the time, Pallas kernels for 0%

commit v1 on v0

v1 whole, which is shorter than its diff:
```python
import functools

import jax
import jax.numpy as jnp
from jax import lax
from jax.experimental import pallas as pl
from jax.experimental.pallas import tpu as pltpu
from jax.sharding import PartitionSpec as P

LOG2E = 1.4426950408889634
TILE = 512
LANES = 128
STATS = 16


def contract(a, b, dims):
    return lax.dot_general(a, b, (dims, ((), ())), preferred_element_type=jnp.float32)


def kernel(
    levels, groups, q_hbm, k_hbm, v_hbm, count_hbm, nk_hbm, nv_hbm, pos_hbm, out_ref,
    q_ref, nk_ref, nv_ref, count_ref, pos_ref, loaded, keys, values, fresh, fresh_keys, fresh_values, wide, place_col, place_row,
    scores, extra, tops, queries, total, peaks,
    hop_out, hop_in, ret_out, ret_in,
    load_sem, fresh_send, fresh_recv, ag_send, ag_recv, hop_send, hop_recv, ret_send, ret_recv,
):
    _, heads, tokens, width = q_ref.shape
    rows = heads * tokens
    slots = keys.shape[1]
    tiles = slots // TILE
    half = levels // 2
    pairs = half // 2
    own_new = nk_ref.shape[1]
    factor = LOG2E * width ** -0.5
    me = lax.axis_index("ctx")
    group = lax.axis_index("qh")

    def level(offset):
        return lax.rem(me + offset + levels, levels)

    def send(src, dst, send_sem, recv_sem, where):
        return pltpu.make_async_remote_copy(
            src_ref=src, dst_ref=dst, send_sem=send_sem, recv_sem=recv_sem,
            device_id=where, device_id_type=pl.DeviceIdType.MESH,
        )

    loads = [
        pltpu.make_async_copy(src, dst, load_sem.at[i])
        for i, (src, dst) in enumerate((
            (q_hbm, q_ref), (nk_hbm, nk_ref), (nv_hbm, nv_ref), (count_hbm, count_ref), (pos_hbm, pos_ref),
            (k_hbm.at[0], loaded), (v_hbm.at[0], values.at[:, 0:width]),
        ))
    ]
    for load in loads:
        load.start()

    barrier = pltpu.get_barrier_semaphore()
    for k in range(pairs):
        for sign in (1, -1):
            pl.semaphore_signal(
                barrier, inc=1, device_id={"ctx": level(sign * (2 * k + 1))}, device_id_type=pl.DeviceIdType.MESH
            )
    for k in range(1, groups):
        pl.semaphore_signal(
            barrier, inc=1, device_id={"qh": lax.rem(group + k, groups)}, device_id_type=pl.DeviceIdType.MESH
        )

    for load in loads[:5]:
        load.wait()
    queries[half - 1, rows:2 * rows, :] = (
        q_ref[0].astype(jnp.float32).reshape(rows, width).astype(jnp.bfloat16)
    )
    wide[...] = jnp.zeros_like(wide)
    wide[0:own_new, :] = nk_ref[0].astype(jnp.float32)
    wide[STATS:STATS + own_new, :] = nv_ref[0].astype(jnp.float32)
    fresh[group] = wide[...].astype(jnp.bfloat16)

    def note_places(j, _):
        for i in range(tokens):
            place_col[pl.ds(j * tokens + i, 1), :] = jnp.full((1, LANES), pos_ref[j * tokens + i], jnp.int32)
        return 0

    lax.fori_loop(0, levels, note_places, 0)
    lane = lax.broadcasted_iota(jnp.int32, (8, LANES), 1)
    row = jnp.full((8, LANES), 1 << 30, jnp.int32)
    for g in range(groups):
        for i in range(own_new):
            place = pos_ref[me * tokens + g * own_new + i]
            row = jnp.where(lane == g * STATS + i, place, row)
    place_row[...] = row

    pl.semaphore_wait(barrier, 2 * pairs + groups - 1)

    own = queries.at[half - 1, rows:2 * rows]

    def right_copy(step, src):
        return send(src, queries.at[step, 0:rows], ag_send.at[0, step], ag_recv.at[0, step], {"ctx": level(1)})

    def left_copy(step, src):
        return send(src, queries.at[step, rows:2 * rows], ag_send.at[1, step], ag_recv.at[1, step], {"ctx": level(-1)})

    right_copy(0, own).start()
    left_copy(0, own).start()

    def fresh_copy(k):
        return send(
            fresh.at[group], fresh.at[group], fresh_send.at[k], fresh_recv.at[group],
            {"qh": lax.rem(group + k, groups)},
        )

    def fresh_arrival(k):
        other = lax.rem(group + k, groups)
        return send(fresh.at[other], fresh.at[other], fresh_send.at[k], fresh_recv.at[other], {"qh": other})

    for k in range(1, groups):
        fresh_copy(k).start()

    count = count_ref[0]
    loads[5].wait()
    loads[6].wait()
    first_key = loaded[0:16, :].astype(jnp.float32)[0:1, :]
    chunk = 256

    def prepare(j, _):
        base = pl.multiple_of(j * chunk, chunk)
        at = pl.ds(base, chunk)
        valid = lax.broadcasted_iota(jnp.int32, (chunk, width), 0) + base < count
        mass = jnp.where(valid, 1.0, 0.0).astype(jnp.bfloat16)
        values[at, width:2 * width] = mass
        values[at, 0:width] = values[at, 0:width] * mass
        chosen = jnp.where(valid, loaded[at, :].astype(jnp.float32), first_key)
        keys[:, at] = chosen.T.astype(jnp.bfloat16)
        return 0

    lax.fori_loop(0, slots // chunk, prepare, 0)

    fresh_keys[...] = jnp.zeros_like(fresh_keys)
    fresh_values[:, 0:width] = jnp.zeros((LANES, width), jnp.bfloat16)
    fresh_values[:, width:2 * width] = jnp.ones((LANES, width), jnp.bfloat16)
    for k in range(1, groups):
        fresh_arrival(k).wait_recv()
    for g in range(groups):
        fresh_keys[g * STATS:(g + 1) * STATS, :] = fresh[g, 0:STATS, :]
        fresh_values[g * STATS:(g + 1) * STATS, 0:width] = fresh[g, STATS:2 * STATS, :]

    def score_tile(step, j):
        at = pl.ds(pl.multiple_of(j * TILE, TILE), TILE)
        made = contract(queries[step], keys[:, at], ((1,), (0,)))
        scores[step % 2, j] = made
        top = tops[...]
        for g in range(TILE // LANES):
            top = jnp.maximum(top, made[:, g * LANES:(g + 1) * LANES])
        tops[...] = top

    def score_start():
        tops[...] = jnp.full(tops.shape, -1e30, jnp.float32)

    def score_end(step):
        made = contract(queries[step], fresh_keys[...], ((1,), (1,)))
        behind = level(-(step + 1))
        ahead = jnp.where(step == half - 1, me, level(step + 1))

        def causal(owner, part):
            place = place_col[pl.ds(pl.multiple_of(owner * tokens, 8), tokens), :]
            place = jnp.concatenate([place] * heads, axis=0)
            limit = jnp.broadcast_to(place_row[0:1, :], place.shape)
            return jnp.where(limit <= place, part, -1e30)

        made = jnp.concatenate([causal(behind, made[0:rows]), causal(ahead, made[rows:])], axis=0)
        extra[step % 2] = made
        top = jnp.max(jnp.maximum(tops[...], made), axis=1, keepdims=True)
        top = top.astype(jnp.bfloat16).astype(jnp.float32)
        peaks[step] = jnp.broadcast_to(top, (2 * rows, LANES))

    def weigh(made, peak):
        return [
            jnp.exp2(made[:, g * LANES:(g + 1) * LANES] * factor - peak)
            for g in range(made.shape[1] // LANES)
        ]

    def weigh_start(step):
        weight = weigh(extra[step % 2], peaks[step] * factor)[0].astype(jnp.bfloat16)
        total[step] = contract(weight, fresh_values[...], ((1,), (0,)))

    def weigh_tile(step, j):
        at = pl.ds(pl.multiple_of(j * TILE, TILE), TILE)
        weight = jnp.concatenate(weigh(scores[step % 2, j], peaks[step] * factor), axis=1).astype(jnp.bfloat16)
        total[step] += contract(weight, values[at, :], ((1,), (0,)))

    eye = lax.broadcasted_iota(jnp.int32, (rows, LANES), 0) == lax.broadcasted_iota(jnp.int32, (rows, LANES), 1)

    def pack(ref, part):
        number, mass, peak = part
        ref[0:rows, :] = number.astype(jnp.bfloat16)
        peak_row = jnp.sum(jnp.where(eye, peak, 0.0), axis=0, keepdims=True)
        mass_row = jnp.sum(jnp.where(eye, mass, 0.0), axis=0, keepdims=True)
        mass_high = mass_row.astype(jnp.bfloat16).astype(jnp.float32)
        line = lax.broadcasted_iota(jnp.int32, (STATS, LANES), 0)
        stats = jnp.where(
            line == 0, peak_row, jnp.where(line == 1, mass_high, jnp.where(line == 2, mass_row - mass_high, 0.0))
        )
        ref[rows:rows + STATS, :] = stats.astype(jnp.bfloat16)

    def unpack(ref):
        number = ref[0:rows, :].astype(jnp.float32)
        stats = ref[rows:rows + STATS, :].astype(jnp.float32)

        def column(line):
            spread = jnp.where(eye, jnp.broadcast_to(line, (rows, LANES)), 0.0)
            return jnp.broadcast_to(jnp.sum(spread, axis=1, keepdims=True), (rows, LANES))

        return number, column(stats[1:2, :] + stats[2:3, :]), column(stats[0:1, :])

    def local(step, side):
        at = slice(side * rows, (side + 1) * rows)
        return total[step, at, 0:width], total[step, at, width:2 * width], peaks[step, at, :]

    def merge(a, b):
        peak = jnp.maximum(a[2], b[2])
        wa = jnp.exp2((a[2] - peak) * factor)
        wb = jnp.exp2((b[2] - peak) * factor)
        return a[0] * wa + b[0] * wb, a[1] * wa + b[1] * wb, peak

    def hop_copy(side, k):
        return send(
            hop_out.at[side, k], hop_in.at[side, k], hop_send.at[side, k], hop_recv.at[side, k],
            {"ctx": level(-1 if side == 0 else 1)},
        )

    def ret_copy(side, k):
        distance = 2 * k + 1
        return send(
            ret_out.at[side, k], ret_in.at[side, k], ret_send.at[side, k], ret_recv.at[side, k],
            {"ctx": level(-distance if side == 0 else distance)},
        )

    def pass_on(side, k):
        pack(hop_out.at[side, k], local(2 * k + 1, side))
        hop_copy(side, k).start()

    def return_pair(side, k):
        hop_copy(side, k).wait_recv()
        pack(ret_out.at[side, k], merge(local(2 * k, side), unpack(hop_in.at[side, k])))
        ret_copy(side, k).start()

    def forward(step):
        right_copy(step, queries.at[step, 0:rows]).wait_recv()

        @pl.when(step < half - 1)
        def _():
            right_copy(step + 1, queries.at[step, 0:rows]).start()
            left_copy(step, queries.at[step, rows:2 * rows]).wait_recv()

        @pl.when(step < half - 2)
        def _():
            left_copy(step + 1, queries.at[step, rows:2 * rows]).start()

    forward(0)
    score_start()

    def first(j, _):
        score_tile(0, j)
        return 0

    lax.fori_loop(0, tiles, first, 0)
    score_end(0)

    def turn(step, _):
        forward(step + 1)
        score_start()
        weigh_start(step)

        def both(j, _):
            score_tile(step + 1, j)
            weigh_tile(step, j)
            return 0

        lax.fori_loop(0, tiles, both, 0)
        score_end(step + 1)

        @pl.when(step % 2 == 1)
        def _():
            pass_on(0, step // 2)
            pass_on(1, step // 2)

        @pl.when((step % 2 == 0) & (step >= 2))
        def _():
            return_pair(0, step // 2 - 1)
            return_pair(1, step // 2 - 1)

        return 0

    lax.fori_loop(0, half - 1, turn, 0)
    pack(ret_out.at[1, pairs - 1], local(half - 2, 1))
    ret_copy(1, pairs - 1).start()
    weigh_start(half - 1)

    def last(j, _):
        weigh_tile(half - 1, j)
        return 0

    lax.fori_loop(0, tiles, last, 0)
    pass_on(0, pairs - 1)
    result = local(half - 1, 1)
    for k in range(pairs - 1):
        for side in (0, 1):
            ret_copy(side, k).wait_recv()
            result = merge(result, unpack(ret_in.at[side, k]))
    return_pair(0, pairs - 1)
    for side in (1, 0):
        ret_copy(side, pairs - 1).wait_recv()
        result = merge(result, unpack(ret_in.at[side, pairs - 1]))
    out_ref[0] = (result[0] / result[1]).reshape(heads, tokens, width).astype(jnp.bfloat16)

    for step in range(half):
        right_copy(step, own).wait_send()
        if step < half - 1:
            left_copy(step, own).wait_send()
    for k in range(1, groups):
        fresh_copy(k).wait_send()
    for k in range(pairs):
        for side in (0, 1):
            ret_copy(side, k).wait_send()
            if (side, k) != (1, pairs - 1):
                hop_copy(side, k).wait_send()


def per_device(queries, cache_keys, cache_values, cache_counts, new_keys, new_values, new_positions):
    levels = lax.axis_size("ctx")
    groups = lax.axis_size("qh")
    _, heads, tokens, width = queries.shape
    slots = cache_keys.shape[1]
    rows = heads * tokens
    half = levels // 2
    pairs = half // 2
    vmem = pl.BlockSpec(memory_space=pltpu.VMEM)
    anywhere = pl.BlockSpec(memory_space=pl.ANY)
    packed = rows + STATS
    dma = pltpu.SemaphoreType.DMA
    scratch = [
        pltpu.VMEM(queries.shape, queries.dtype),
        pltpu.VMEM(new_keys.shape, new_keys.dtype),
        pltpu.VMEM(new_values.shape, new_values.dtype),
        pltpu.SMEM(cache_counts.shape, cache_counts.dtype),
        pltpu.SMEM(new_positions.shape, new_positions.dtype),
        pltpu.VMEM((slots, width), jnp.bfloat16),
        pltpu.VMEM((width, slots), jnp.bfloat16),
        pltpu.VMEM((slots, 2 * width), jnp.bfloat16),
        pltpu.VMEM((groups, 2 * STATS, width), jnp.bfloat16),
        pltpu.VMEM((LANES, width), jnp.bfloat16),
        pltpu.VMEM((LANES, 2 * width), jnp.bfloat16),
        pltpu.VMEM((2 * STATS, width), jnp.float32),
        pltpu.VMEM((levels * tokens, LANES), jnp.int32),
        pltpu.VMEM((8, LANES), jnp.int32),
        pltpu.VMEM((2, slots // TILE, 2 * rows, TILE), jnp.float32),
        pltpu.VMEM((2, 2 * rows, LANES), jnp.float32),
        pltpu.VMEM((2 * rows, LANES), jnp.float32),
        pltpu.VMEM((half, 2 * rows, width), jnp.bfloat16),
        pltpu.VMEM((half, 2 * rows, 2 * width), jnp.float32),
        pltpu.VMEM((half, 2 * rows, LANES), jnp.float32),
        pltpu.VMEM((2, pairs, packed, width), jnp.bfloat16),
        pltpu.VMEM((2, pairs, packed, width), jnp.bfloat16),
        pltpu.VMEM((2, pairs, packed, width), jnp.bfloat16),
        pltpu.VMEM((2, pairs, packed, width), jnp.bfloat16),
        dma((7,)),
        dma((groups,)),
        dma((groups,)),
        dma((2, half)),
        dma((2, half)),
        dma((2, pairs)),
        dma((2, pairs)),
        dma((2, pairs)),
        dma((2, pairs)),
    ]
    return pl.pallas_call(
        functools.partial(kernel, levels, groups),
        out_shape=jax.ShapeDtypeStruct(queries.shape, queries.dtype),
        in_specs=[anywhere] * 7,
        out_specs=vmem,
        scratch_shapes=scratch,
        compiler_params=pltpu.CompilerParams(
            collective_id=0, has_side_effects=True, vmem_limit_bytes=60 * 1024 * 1024
        ),
        cost_estimate=pl.CostEstimate(
            flops=4 * levels * rows * slots * width,
            bytes_accessed=4 * slots * width,
            transcendentals=levels * rows * slots,
        ),
        name="ring_attention",
    )(queries, cache_keys, cache_values, cache_counts, new_keys, new_values, new_positions)


def solution(mesh):
    placed = (
        P("kv", "qh", "ctx", None),
        P("kv", "ctx", None),
        P("kv", "ctx", None),
        P("ctx"),
        P("kv", ("ctx", "qh"), None),
        P("kv", ("ctx", "qh"), None),
        P(),
    )
    return jax.shard_map(
        per_device,
        mesh=mesh,
        in_specs=placed,
        out_specs=P("kv", "qh", "ctx", None),
        check_vma=False,
    )
```

time: 461 us -> 67.4 us (0.15)
  the two profiles are of different devices: /device:TPU:24 before, /device:TPU:40 now
where the time goes in v1:
time: 67.4 us; the launch traced here: 67.2 us
  Pallas kernels  65.2 us (97%)
  local copies, waits for them, and re-layouts  1.35 us (2%)
    pallas_call x1, Pallas kernels, per_device(): pl.pallas_call(functools.partial(kernel, levels, groups), out_shape=jax.S...  65.2 us
    unnamed x1, local copies, waits for them, and re-layouts  1.35 us

profile of v1, /device:TPU:40, one launch (start us, length us, event | category | flops | bytes accessed | tf_op | source)
XLA Modules:
  0.0 67.2 jit_solution(11820022565176062875)
XLA Ops:
  0.7 65.2 %ring_attention.1 = bf16[1,4,24,128]{3,2,1,0:T(8,128)(2,1)} custom-call(bf16[1,4,24,128]{3,2,1,0:T(8,128)(2,1)} %q_hbm.1, bf16[1,4096,128]{2,1,0:T(8,128)(2,1)} %k_hbm.1, bf16[1,4096,128]{2,1,0:T(8,128)(2,1)} %v_hbm.1, s32[1]{0:T(128)S(6)} %copy.9.count_hbm, bf16[1,6,128]{2,1,0:T(8,128)(2,1)} %nk_hbm.1, bf16[1,6,128]{2,1,0:T(8,128)(2,1)} %nv_hbm.1, s32[384]{0:T(512)} %pos_hbm.1), custom_call_target="tpu_custom_call" | custom-call | flops 3221225472 | bytes 2097152 | tf_op jit(solution)/shard_map/ring_attention/pallas_call | solution.py:375
  65.9 1.3 %copy.10 = bf16[1,4,24,128]{3,2,1,0:T(8,128)(2,1)} copy(bf16[1,4,24,128]{3,2,1,0:T(8,128)(2,1)} %ring_attention.1) | data formatting | bytes 49152

commit v2 on v1

--- a/solution.py
+++ b/solution.py
@@ -8,7 +8,7 @@
 from jax.sharding import PartitionSpec as P
 
 LOG2E = 1.4426950408889634
-TILE = 512
+TILE = 2048
 LANES = 128
 STATS = 16
 

time: 67.4 us -> 61.8 us (0.917)
  the two profiles are of different devices: /device:TPU:40 before, /device:TPU:24 now
where the time goes in v2:
time: 61.8 us; the launch traced here: 61.1 us
  Pallas kernels  59.1 us (96%)
  local copies, waits for them, and re-layouts  1.35 us (2%)
  between operations  0.66 us (1%)
    pallas_call x1, Pallas kernels, per_device(): pl.pallas_call(functools.partial(kernel, levels, groups), out_shape=jax.S...  59.1 us
    unnamed x1, local copies, waits for them, and re-layouts  1.35 us

profile of v2, /device:TPU:24, one launch (start us, length us, event | category | flops | bytes accessed | tf_op | source)
XLA Modules:
  0.0 61.1 jit_solution(4190923779504660494)
XLA Ops:
  0.7 59.1 %ring_attention.1 = bf16[1,4,24,128]{3,2,1,0:T(8,128)(2,1)} custom-call(bf16[1,4,24,128]{3,2,1,0:T(8,128)(2,1)} %q_hbm.1, bf16[1,4096,128]{2,1,0:T(8,128)(2,1)} %k_hbm.1, bf16[1,4096,128]{2,1,0:T(8,128)(2,1)} %v_hbm.1, s32[1]{0:T(128)S(6)} %copy.9.count_hbm, bf16[1,6,128]{2,1,0:T(8,128)(2,1)} %nk_hbm.1, bf16[1,6,128]{2,1,0:T(8,128)(2,1)} %nv_hbm.1, s32[384]{0:T(512)} %pos_hbm.1), custom_call_target="tpu_custom_call" | custom-call | flops 3221225472 | bytes 2097152 | tf_op jit(solution)/shard_map/ring_attention/pallas_call | solution.py:375
  59.7 1.3 %copy.10 = bf16[1,4,24,128]{3,2,1,0:T(8,128)(2,1)} copy(bf16[1,4,24,128]{3,2,1,0:T(8,128)(2,1)} %ring_attention.1) | data formatting | bytes 49152

commit v3 on v2

--- a/solution.py
+++ b/solution.py
@@ -21,15 +21,15 @@
     levels, groups, q_hbm, k_hbm, v_hbm, count_hbm, nk_hbm, nv_hbm, pos_hbm, out_ref,
     q_ref, nk_ref, nv_ref, count_ref, pos_ref, loaded, keys, values, fresh, fresh_keys, fresh_values, wide, place_col, place_row,
     scores, extra, tops, queries, total, peaks,
-    hop_out, hop_in, ret_out, ret_in,
-    load_sem, fresh_send, fresh_recv, ag_send, ag_recv, hop_send, hop_recv, ret_send, ret_recv,
+    sent, landed,
+    load_sem, fresh_send, fresh_recv, ag_send, ag_recv, back_send, back_recv,
 ):
     _, heads, tokens, width = q_ref.shape
     rows = heads * tokens
     slots = keys.shape[1]
     tiles = slots // TILE
     half = levels // 2
-    pairs = half // 2
+    near = half // 2
     own_new = nk_ref.shape[1]
     factor = LOG2E * width ** -0.5
     me = lax.axis_index("ctx")
@@ -55,11 +55,8 @@
         load.start()
 
     barrier = pltpu.get_barrier_semaphore()
-    for k in range(pairs):
-        for sign in (1, -1):
-            pl.semaphore_signal(
-                barrier, inc=1, device_id={"ctx": level(sign * (2 * k + 1))}, device_id_type=pl.DeviceIdType.MESH
-            )
+    for distance in (1, -1, near + 1, -near - 1):
+        pl.semaphore_signal(barrier, inc=1, device_id={"ctx": level(distance)}, device_id_type=pl.DeviceIdType.MESH)
     for k in range(1, groups):
         pl.semaphore_signal(
             barrier, inc=1, device_id={"qh": lax.rem(group + k, groups)}, device_id_type=pl.DeviceIdType.MESH
@@ -89,7 +86,7 @@
             row = jnp.where(lane == g * STATS + i, place, row)
     place_row[...] = row
 
-    pl.semaphore_wait(barrier, 2 * pairs + groups - 1)
+    pl.semaphore_wait(barrier, 4 + groups - 1)
 
     own = queries.at[half - 1, rows:2 * rows]
 
@@ -221,27 +218,21 @@
         wb = jnp.exp2((b[2] - peak) * factor)
         return a[0] * wa + b[0] * wb, a[1] * wa + b[1] * wb, peak
 
-    def hop_copy(side, k):
+    def back_copy(side, step):
+        hop = jnp.where(step == near, near + 1, 1)
         return send(
-            hop_out.at[side, k], hop_in.at[side, k], hop_send.at[side, k], hop_recv.at[side, k],
-            {"ctx": level(-1 if side == 0 else 1)},
-        )
-
-    def ret_copy(side, k):
-        distance = 2 * k + 1
-        return send(
-            ret_out.at[side, k], ret_in.at[side, k], ret_send.at[side, k], ret_recv.at[side, k],
-            {"ctx": level(-distance if side == 0 else distance)},
-        )
-
-    def pass_on(side, k):
-        pack(hop_out.at[side, k], local(2 * k + 1, side))
-        hop_copy(side, k).start()
-
-    def return_pair(side, k):
-        hop_copy(side, k).wait_recv()
-        pack(ret_out.at[side, k], merge(local(2 * k, side), unpack(hop_in.at[side, k])))
-        ret_copy(side, k).start()
+            sent.at[side, step], landed.at[side, step], back_send.at[side, step], back_recv.at[side, step],
+            {"ctx": level(-hop if side == 0 else hop)},
+        )
+
+    def pass_first(side, step):
+        pack(sent.at[side, step], local(step, side))
+        back_copy(side, step).start()
+
+    def pass_merged(side, step):
+        back_copy(side, step + 1).wait_recv()
+        pack(sent.at[side, step], merge(local(step, side), unpack(landed.at[side, step + 1])))
+        back_copy(side, step).start()
 
     def forward(step):
         right_copy(step, queries.at[step, 0:rows]).wait_recv()
@@ -278,21 +269,20 @@
         lax.fori_loop(0, tiles, both, 0)
         score_end(step + 1)
 
-        @pl.when(step % 2 == 1)
+        @pl.when(step == near - 1)
         def _():
-            pass_on(0, step // 2)
-            pass_on(1, step // 2)
-
-        @pl.when((step % 2 == 0) & (step >= 2))
+            pass_first(0, near - 1)
+            pass_first(1, near - 1)
+
+        @pl.when(step >= near)
         def _():
-            return_pair(0, step // 2 - 1)
-            return_pair(1, step // 2 - 1)
+            pass_merged(0, half - 2 - step)
+            pass_merged(1, half - 2 - step)
 
         return 0
 
     lax.fori_loop(0, half - 1, turn, 0)
-    pack(ret_out.at[1, pairs - 1], local(half - 2, 1))
-    ret_copy(1, pairs - 1).start()
+    pass_first(1, half - 2)
     weigh_start(half - 1)
 
     def last(j, _):
@@ -300,29 +290,26 @@
         return 0
 
     lax.fori_loop(0, tiles, last, 0)
-    pass_on(0, pairs - 1)
+    pass_first(0, half - 1)
     result = local(half - 1, 1)
-    for k in range(pairs - 1):
-        for side in (0, 1):
-            ret_copy(side, k).wait_recv()
-            result = merge(result, unpack(ret_in.at[side, k]))
-    return_pair(0, pairs - 1)
-    for side in (1, 0):
-        ret_copy(side, pairs - 1).wait_recv()
-        result = merge(result, unpack(ret_in.at[side, pairs - 1]))
+    for step in range(half - 3, near - 1, -1):
+        pass_merged(1, step)
+        pass_merged(0, step + 1)
+    pass_merged(0, near)
+    for step in (0, near):
+        for side in (1, 0):
+            back_copy(side, step).wait_recv()
+            result = merge(result, unpack(landed.at[side, step]))
     out_ref[0] = (result[0] / result[1]).reshape(heads, tokens, width).astype(jnp.bfloat16)
 
     for step in range(half):
         right_copy(step, own).wait_send()
+        back_copy(0, step).wait_send()
         if step < half - 1:
             left_copy(step, own).wait_send()
+            back_copy(1, step).wait_send()
     for k in range(1, groups):
         fresh_copy(k).wait_send()
-    for k in range(pairs):
-        for side in (0, 1):
-            ret_copy(side, k).wait_send()
-            if (side, k) != (1, pairs - 1):
-                hop_copy(side, k).wait_send()
 
 
 def per_device(queries, cache_keys, cache_values, cache_counts, new_keys, new_values, new_positions):
@@ -332,7 +319,6 @@
     slots = cache_keys.shape[1]
     rows = heads * tokens
     half = levels // 2
-    pairs = half // 2
     vmem = pl.BlockSpec(memory_space=pltpu.VMEM)
     anywhere = pl.BlockSpec(memory_space=pl.ANY)
     packed = rows + STATS
@@ -358,19 +344,15 @@
         pltpu.VMEM((half, 2 * rows, width), jnp.bfloat16),
         pltpu.VMEM((half, 2 * rows, 2 * width), jnp.float32),
         pltpu.VMEM((half, 2 * rows, LANES), jnp.float32),
-        pltpu.VMEM((2, pairs, packed, width), jnp.bfloat16),
-        pltpu.VMEM((2, pairs, packed, width), jnp.bfloat16),
-        pltpu.VMEM((2, pairs, packed, width), jnp.bfloat16),
-        pltpu.VMEM((2, pairs, packed, width), jnp.bfloat16),
+        pltpu.VMEM((2, half, packed, width), jnp.bfloat16),
+        pltpu.VMEM((2, half, packed, width), jnp.bfloat16),
         dma((7,)),
         dma((groups,)),
         dma((groups,)),
         dma((2, half)),
         dma((2, half)),
-        dma((2, pairs)),
-        dma((2, pairs)),
-        dma((2, pairs)),
-        dma((2, pairs)),
+        dma((2, half)),
+        dma((2, half)),
     ]
     return pl.pallas_call(
         functools.partial(kernel, levels, groups),

time: 61.8 us -> 62.6 us (1.013)
  Pallas kernels: 59.1 us -> 60.4 us
    pallas_call x1, Pallas kernels: 59.1 us -> 60.4 us  [per_device(): pl.pallas_call(functools.partial(kernel, levels, groups), out_shape=jax.S...]
where the time goes in v3:
time: 62.6 us; the launch traced here: 62.4 us
  Pallas kernels  60.4 us (96%)
  local copies, waits for them, and re-layouts  1.35 us (2%)
  between operations  0.66 us (1%)
    pallas_call x1, Pallas kernels, per_device(): pl.pallas_call(functools.partial(kernel, levels, groups), out_shape=jax.S...  60.4 us
    unnamed x1, local copies, waits for them, and re-layouts  1.35 us

profile of v3, /device:TPU:24, one launch (start us, length us, event | category | flops | bytes accessed | tf_op | source)
XLA Modules:
  0.0 62.4 jit_solution(11011691860828856649)
XLA Ops:
  0.7 60.4 %ring_attention.1 = bf16[1,4,24,128]{3,2,1,0:T(8,128)(2,1)} custom-call(bf16[1,4,24,128]{3,2,1,0:T(8,128)(2,1)} %q_hbm.1, bf16[1,4096,128]{2,1,0:T(8,128)(2,1)} %k_hbm.1, bf16[1,4096,128]{2,1,0:T(8,128)(2,1)} %v_hbm.1, s32[1]{0:T(128)S(6)} %copy.9.count_hbm, bf16[1,6,128]{2,1,0:T(8,128)(2,1)} %nk_hbm.1, bf16[1,6,128]{2,1,0:T(8,128)(2,1)} %nv_hbm.1, s32[384]{0:T(512)} %pos_hbm.1), custom_call_target="tpu_custom_call" | custom-call | flops 3221225472 | bytes 2097152 | tf_op jit(solution)/shard_map/ring_attention/pallas_call | solution.py:357
  61.1 1.3 %copy.10 = bf16[1,4,24,128]{3,2,1,0:T(8,128)(2,1)} copy(bf16[1,4,24,128]{3,2,1,0:T(8,128)(2,1)} %ring_attention.1) | data formatting | bytes 49152

commit v4 on v3

--- a/solution.py
+++ b/solution.py
@@ -8,7 +8,7 @@
 from jax.sharding import PartitionSpec as P
 
 LOG2E = 1.4426950408889634
-TILE = 2048
+TILE = 1024
 LANES = 128
 STATS = 16
 
@@ -30,6 +30,7 @@
     tiles = slots // TILE
     half = levels // 2
     near = half // 2
+    quarters = 4
     own_new = nk_ref.shape[1]
     factor = LOG2E * width ** -0.5
     me = lax.axis_index("ctx")
@@ -55,7 +56,8 @@
         load.start()
 
     barrier = pltpu.get_barrier_semaphore()
-    for distance in (1, -1, near + 1, -near - 1):
+    partners = (1, -1, near + 1, -near - 1, near, -near, half - 1, 1 - half, half)
+    for distance in partners:
         pl.semaphore_signal(barrier, inc=1, device_id={"ctx": level(distance)}, device_id_type=pl.DeviceIdType.MESH)
     for k in range(1, groups):
         pl.semaphore_signal(
@@ -64,7 +66,7 @@
 
     for load in loads[:5]:
         load.wait()
-    queries[half - 1, rows:2 * rows, :] = (
+    queries[near - 1, 3 * rows:4 * rows, :] = (
         q_ref[0].astype(jnp.float32).reshape(rows, width).astype(jnp.bfloat16)
     )
     wide[...] = jnp.zeros_like(wide)
@@ -86,18 +88,21 @@
             row = jnp.where(lane == g * STATS + i, place, row)
     place_row[...] = row
 
-    pl.semaphore_wait(barrier, 4 + groups - 1)
-
-    own = queries.at[half - 1, rows:2 * rows]
-
-    def right_copy(step, src):
-        return send(src, queries.at[step, 0:rows], ag_send.at[0, step], ag_recv.at[0, step], {"ctx": level(1)})
-
-    def left_copy(step, src):
-        return send(src, queries.at[step, rows:2 * rows], ag_send.at[1, step], ag_recv.at[1, step], {"ctx": level(-1)})
-
-    right_copy(0, own).start()
-    left_copy(0, own).start()
+    pl.semaphore_wait(barrier, len(partners) + groups - 1)
+
+    own = queries.at[near - 1, 3 * rows:4 * rows]
+
+    def part(quarter):
+        return slice(quarter * rows, (quarter + 1) * rows)
+
+    def query_copy(quarter, step, src, hop):
+        return send(
+            src, queries.at[step, part(quarter)], ag_send.at[quarter, step], ag_recv.at[quarter, step],
+            {"ctx": level(hop if quarter % 2 == 0 else -hop)},
+        )
+
+    for quarter in range(quarters):
+        query_copy(quarter, 0, own, near + 1 if quarter >= 2 else 1).start()
 
     def fresh_copy(k):
         return send(
@@ -116,7 +121,7 @@
     loads[5].wait()
     loads[6].wait()
     first_key = loaded[0:16, :].astype(jnp.float32)[0:1, :]
-    chunk = 256
+    chunk = 1024
 
     def prepare(j, _):
         base = pl.multiple_of(j * chunk, chunk)
@@ -154,20 +159,22 @@
 
     def score_end(step):
         made = contract(queries[step], fresh_keys[...], ((1,), (1,)))
-        behind = level(-(step + 1))
-        ahead = jnp.where(step == half - 1, me, level(step + 1))
-
-        def causal(owner, part):
+        owners = (
+            level(-(step + 1)), level(step + 1), level(-(step + near + 1)),
+            jnp.where(step == near - 1, me, level(step + near + 1)),
+        )
+
+        def causal(owner, made):
             place = place_col[pl.ds(pl.multiple_of(owner * tokens, 8), tokens), :]
             place = jnp.concatenate([place] * heads, axis=0)
             limit = jnp.broadcast_to(place_row[0:1, :], place.shape)
-            return jnp.where(limit <= place, part, -1e30)
-
-        made = jnp.concatenate([causal(behind, made[0:rows]), causal(ahead, made[rows:])], axis=0)
+            return jnp.where(limit <= place, made, -1e30)
+
+        made = jnp.concatenate([causal(owners[q], made[part(q)]) for q in range(quarters)], axis=0)
         extra[step % 2] = made
         top = jnp.max(jnp.maximum(tops[...], made), axis=1, keepdims=True)
         top = top.astype(jnp.bfloat16).astype(jnp.float32)
-        peaks[step] = jnp.broadcast_to(top, (2 * rows, LANES))
+        peaks[step] = jnp.broadcast_to(top, (quarters * rows, LANES))
 
     def weigh(made, peak):
         return [
@@ -186,8 +193,8 @@
 
     eye = lax.broadcasted_iota(jnp.int32, (rows, LANES), 0) == lax.broadcasted_iota(jnp.int32, (rows, LANES), 1)
 
-    def pack(ref, part):
-        number, mass, peak = part
+    def pack(ref, summed):
+        number, mass, peak = summed
         ref[0:rows, :] = number.astype(jnp.bfloat16)
         peak_row = jnp.sum(jnp.where(eye, peak, 0.0), axis=0, keepdims=True)
         mass_row = jnp.sum(jnp.where(eye, mass, 0.0), axis=0, keepdims=True)
@@ -208,8 +215,8 @@
 
         return number, column(stats[1:2, :] + stats[2:3, :]), column(stats[0:1, :])
 
-    def local(step, side):
-        at = slice(side * rows, (side + 1) * rows)
+    def local(step, quarter):
+        at = part(quarter)
         return total[step, at, 0:width], total[step, at, width:2 * width], peaks[step, at, :]
 
     def merge(a, b):
@@ -218,33 +225,46 @@
         wb = jnp.exp2((b[2] - peak) * factor)
         return a[0] * wa + b[0] * wb, a[1] * wa + b[1] * wb, peak
 
-    def back_copy(side, step):
-        hop = jnp.where(step == near, near + 1, 1)
+    last_step = (near - 1, near - 1, near - 1, near - 2)
+    furthest = (near, near, half, half - 1)
+
+    def back_copy(quarter, step):
+        hop = jnp.where(step == last_step[quarter], -furthest[quarter], 1)
         return send(
-            sent.at[side, step], landed.at[side, step], back_send.at[side, step], back_recv.at[side, step],
-            {"ctx": level(-hop if side == 0 else hop)},
-        )
-
-    def pass_first(side, step):
-        pack(sent.at[side, step], local(step, side))
-        back_copy(side, step).start()
-
-    def pass_merged(side, step):
-        back_copy(side, step + 1).wait_recv()
-        pack(sent.at[side, step], merge(local(step, side), unpack(landed.at[side, step + 1])))
-        back_copy(side, step).start()
+            sent.at[quarter, step], landed.at[quarter, step], back_send.at[quarter, step],
+            back_recv.at[quarter, step], {"ctx": level(hop if quarter % 2 == 0 else -hop)},
+        )
+
+    def pass_first(quarter):
+        pack(sent.at[quarter, 0], local(0, quarter))
+        back_copy(quarter, 0).start()
+
+    def pass_merged(quarter, step):
+        back_copy(quarter, step - 1).wait_recv()
+        pack(sent.at[quarter, step], merge(local(step, quarter), unpack(landed.at[quarter, step - 1])))
+        back_copy(quarter, step).start()
+
+    def arrive(quarter, step):
+        query_copy(quarter, step, own, 1).wait_recv()
+
+    def follow(quarter, step):
+        query_copy(quarter, step + 1, queries.at[step, part(quarter)], 1).start()
 
     def forward(step):
-        right_copy(step, queries.at[step, 0:rows]).wait_recv()
-
-        @pl.when(step < half - 1)
+        for quarter in (0, 1, 2):
+            arrive(quarter, step)
+
+            @pl.when(step < near - 1)
+            def _():
+                follow(quarter, step)
+
+        @pl.when(step < near - 1)
         def _():
-            right_copy(step + 1, queries.at[step, 0:rows]).start()
-            left_copy(step, queries.at[step, rows:2 * rows]).wait_recv()
-
-        @pl.when(step < half - 2)
+            arrive(3, step)
+
+        @pl.when(step < near - 2)
         def _():
-            left_copy(step + 1, queries.at[step, rows:2 * rows]).start()
+            follow(3, step)
 
     forward(0)
     score_start()
@@ -269,45 +289,38 @@
         lax.fori_loop(0, tiles, both, 0)
         score_end(step + 1)
 
-        @pl.when(step == near - 1)
+        @pl.when(step == 0)
         def _():
-            pass_first(0, near - 1)
-            pass_first(1, near - 1)
-
-        @pl.when(step >= near)
+            for quarter in range(quarters):
+                pass_first(quarter)
+
+        @pl.when(step > 0)
         def _():
-            pass_merged(0, half - 2 - step)
-            pass_merged(1, half - 2 - step)
+            for quarter in range(quarters):
+                pass_merged(quarter, step)
 
         return 0
 
-    lax.fori_loop(0, half - 1, turn, 0)
-    pass_first(1, half - 2)
-    weigh_start(half - 1)
+    lax.fori_loop(0, near - 1, turn, 0)
+    weigh_start(near - 1)
 
     def last(j, _):
-        weigh_tile(half - 1, j)
+        weigh_tile(near - 1, j)
         return 0
 
     lax.fori_loop(0, tiles, last, 0)
-    pass_first(0, half - 1)
-    result = local(half - 1, 1)
-    for step in range(half - 3, near - 1, -1):
-        pass_merged(1, step)
-        pass_merged(0, step + 1)
-    pass_merged(0, near)
-    for step in (0, near):
-        for side in (1, 0):
-            back_copy(side, step).wait_recv()
-            result = merge(result, unpack(landed.at[side, step]))
+    for quarter in (2, 0, 1):
+        pass_merged(quarter, near - 1)
+    result = local(near - 1, 3)
+    for quarter in (3, 0, 1, 2):
+        back_copy(quarter, last_step[quarter]).wait_recv()
+        result = merge(result, unpack(landed.at[quarter, last_step[quarter]]))
     out_ref[0] = (result[0] / result[1]).reshape(heads, tokens, width).astype(jnp.bfloat16)
 
-    for step in range(half):
-        right_copy(step, own).wait_send()
-        back_copy(0, step).wait_send()
-        if step < half - 1:
-            left_copy(step, own).wait_send()
-            back_copy(1, step).wait_send()
+    for quarter in range(quarters):
+        for step in range(last_step[quarter] + 1):
+            query_copy(quarter, step, own, 1).wait_send()
+            back_copy(quarter, step).wait_send()
     for k in range(1, groups):
         fresh_copy(k).wait_send()
 
@@ -318,7 +331,7 @@
     _, heads, tokens, width = queries.shape
     slots = cache_keys.shape[1]
     rows = heads * tokens
-    half = levels // 2
+    near = levels // 4
     vmem = pl.BlockSpec(memory_space=pltpu.VMEM)
     anywhere = pl.BlockSpec(memory_space=pl.ANY)
     packed = rows + STATS
@@ -338,21 +351,21 @@
         pltpu.VMEM((2 * STATS, width), jnp.float32),
         pltpu.VMEM((levels * tokens, LANES), jnp.int32),
         pltpu.VMEM((8, LANES), jnp.int32),
-        pltpu.VMEM((2, slots // TILE, 2 * rows, TILE), jnp.float32),
-        pltpu.VMEM((2, 2 * rows, LANES), jnp.float32),
-        pltpu.VMEM((2 * rows, LANES), jnp.float32),
-        pltpu.VMEM((half, 2 * rows, width), jnp.bfloat16),
-        pltpu.VMEM((half, 2 * rows, 2 * width), jnp.float32),
-        pltpu.VMEM((half, 2 * rows, LANES), jnp.float32),
-        pltpu.VMEM((2, half, packed, width), jnp.bfloat16),
-        pltpu.VMEM((2, half, packed, width), jnp.bfloat16),
+        pltpu.VMEM((2, slots // TILE, 4 * rows, TILE), jnp.float32),
+        pltpu.VMEM((2, 4 * rows, LANES), jnp.float32),
+        pltpu.VMEM((4 * rows, LANES), jnp.float32),
+        pltpu.VMEM((near, 4 * rows, width), jnp.bfloat16),
+        pltpu.VMEM((near, 4 * rows, 2 * width), jnp.float32),
+        pltpu.VMEM((near, 4 * rows, LANES), jnp.float32),
+        pltpu.VMEM((4, near, packed, width), jnp.bfloat16),
+        pltpu.VMEM((4, near, packed, width), jnp.bfloat16),
         dma((7,)),
         dma((groups,)),
         dma((groups,)),
-        dma((2, half)),
-        dma((2, half)),
-        dma((2, half)),
-        dma((2, half)),
+        dma((4, near)),
+        dma((4, near)),
+        dma((4, near)),
+        dma((4, near)),
     ]
     return pl.pallas_call(
         functools.partial(kernel, levels, groups),

time: 62.6 us -> 57.4 us (0.917)
  the two profiles are of different devices: /device:TPU:24 before, /device:TPU:8 now
where the time goes in v4:
time: 57.4 us; the launch traced here: 57.2 us
  Pallas kernels  55.1 us (96%)
  local copies, waits for them, and re-layouts  1.35 us (2%)
  between operations  0.66 us (1%)
    pallas_call x1, Pallas kernels, per_device(): pl.pallas_call(functools.partial(kernel, levels, groups), out_shape=jax.S...  55.1 us
    unnamed x1, local copies, waits for them, and re-layouts  1.35 us

profile of v4, /device:TPU:8, one launch (start us, length us, event | category | flops | bytes accessed | tf_op | source)
XLA Modules:
  0.0 57.2 jit_solution(9142221381729746889)
XLA Ops:
  0.7 55.1 %ring_attention.1 = bf16[1,4,24,128]{3,2,1,0:T(8,128)(2,1)} custom-call(bf16[1,4,24,128]{3,2,1,0:T(8,128)(2,1)} %q_hbm.1, bf16[1,4096,128]{2,1,0:T(8,128)(2,1)} %k_hbm.1, bf16[1,4096,128]{2,1,0:T(8,128)(2,1)} %v_hbm.1, s32[1]{0:T(128)S(6)} %copy.9.count_hbm, bf16[1,6,128]{2,1,0:T(8,128)(2,1)} %nk_hbm.1, bf16[1,6,128]{2,1,0:T(8,128)(2,1)} %nv_hbm.1, s32[384]{0:T(512)} %pos_hbm.1), custom_call_target="tpu_custom_call" | custom-call | flops 3221225472 | bytes 2097152 | tf_op jit(solution)/shard_map/ring_attention/pallas_call | solution.py:370
  55.8 1.3 %copy.10 = bf16[1,4,24,128]{3,2,1,0:T(8,128)(2,1)} copy(bf16[1,4,24,128]{3,2,1,0:T(8,128)(2,1)} %ring_attention.1) | data formatting | bytes 49152

commit v5 on v4

--- a/solution.py
+++ b/solution.py
@@ -20,7 +20,7 @@
 def kernel(
     levels, groups, q_hbm, k_hbm, v_hbm, count_hbm, nk_hbm, nv_hbm, pos_hbm, out_ref,
     q_ref, nk_ref, nv_ref, count_ref, pos_ref, loaded, keys, values, fresh, fresh_keys, fresh_values, wide, place_col, place_row,
-    scores, extra, tops, queries, total, peaks,
+    scores_even, scores_odd, extra, tops, queries, total, peaks,
     sent, landed,
     load_sem, fresh_send, fresh_recv, ag_send, ag_recv, back_send, back_recv,
 ):
@@ -145,10 +145,12 @@
         fresh_keys[g * STATS:(g + 1) * STATS, :] = fresh[g, 0:STATS, :]
         fresh_values[g * STATS:(g + 1) * STATS, 0:width] = fresh[g, STATS:2 * STATS, :]
 
+    scores = (scores_even, scores_odd)
+
     def score_tile(step, j):
         at = pl.ds(pl.multiple_of(j * TILE, TILE), TILE)
         made = contract(queries[step], keys[:, at], ((1,), (0,)))
-        scores[step % 2, j] = made
+        scores[step % 2][j] = made
         top = tops[...]
         for g in range(TILE // LANES):
             top = jnp.maximum(top, made[:, g * LANES:(g + 1) * LANES])
@@ -161,7 +163,7 @@
         made = contract(queries[step], fresh_keys[...], ((1,), (1,)))
         owners = (
             level(-(step + 1)), level(step + 1), level(-(step + near + 1)),
-            jnp.where(step == near - 1, me, level(step + near + 1)),
+            me if step == near - 1 else level(step + near + 1),
         )
 
         def causal(owner, made):
@@ -188,7 +190,7 @@
 
     def weigh_tile(step, j):
         at = pl.ds(pl.multiple_of(j * TILE, TILE), TILE)
-        weight = jnp.concatenate(weigh(scores[step % 2, j], peaks[step] * factor), axis=1).astype(jnp.bfloat16)
+        weight = jnp.concatenate(weigh(scores[step % 2][j], peaks[step] * factor), axis=1).astype(jnp.bfloat16)
         total[step] += contract(weight, values[at, :], ((1,), (0,)))
 
     eye = lax.broadcasted_iota(jnp.int32, (rows, LANES), 0) == lax.broadcasted_iota(jnp.int32, (rows, LANES), 1)
@@ -229,7 +231,7 @@
     furthest = (near, near, half, half - 1)
 
     def back_copy(quarter, step):
-        hop = jnp.where(step == last_step[quarter], -furthest[quarter], 1)
+        hop = -furthest[quarter] if step == last_step[quarter] else 1
         return send(
             sent.at[quarter, step], landed.at[quarter, step], back_send.at[quarter, step],
             back_recv.at[quarter, step], {"ctx": level(hop if quarter % 2 == 0 else -hop)},
@@ -251,20 +253,11 @@
         query_copy(quarter, step + 1, queries.at[step, part(quarter)], 1).start()
 
     def forward(step):
-        for quarter in (0, 1, 2):
-            arrive(quarter, step)
-
-            @pl.when(step < near - 1)
-            def _():
+        for quarter in range(quarters):
+            if step <= last_step[quarter]:
+                arrive(quarter, step)
+            if step < last_step[quarter]:
                 follow(quarter, step)
-
-        @pl.when(step < near - 1)
-        def _():
-            arrive(3, step)
-
-        @pl.when(step < near - 2)
-        def _():
-            follow(3, step)
 
     forward(0)
     score_start()
@@ -276,7 +269,7 @@
     lax.fori_loop(0, tiles, first, 0)
     score_end(0)
 
-    def turn(step, _):
+    for step in range(near - 1):
         forward(step + 1)
         score_start()
         weigh_start(step)
@@ -288,20 +281,12 @@
 
         lax.fori_loop(0, tiles, both, 0)
         score_end(step + 1)
-
-        @pl.when(step == 0)
-        def _():
-            for quarter in range(quarters):
+        for quarter in range(quarters):
+            if step == 0:
                 pass_first(quarter)
-
-        @pl.when(step > 0)
-        def _():
-            for quarter in range(quarters):
+            else:
                 pass_merged(quarter, step)
 
-        return 0
-
-    lax.fori_loop(0, near - 1, turn, 0)
     weigh_start(near - 1)
 
     def last(j, _):
@@ -351,7 +336,8 @@
         pltpu.VMEM((2 * STATS, width), jnp.float32),
         pltpu.VMEM((levels * tokens, LANES), jnp.int32),
         pltpu.VMEM((8, LANES), jnp.int32),
-        pltpu.VMEM((2, slots // TILE, 4 * rows, TILE), jnp.float32),
+        pltpu.VMEM((slots // TILE, 4 * rows, TILE), jnp.float32),
+        pltpu.VMEM((slots // TILE, 4 * rows, TILE), jnp.float32),
         pltpu.VMEM((2, 4 * rows, LANES), jnp.float32),
         pltpu.VMEM((4 * rows, LANES), jnp.float32),
         pltpu.VMEM((near, 4 * rows, width), jnp.bfloat16),

time: 57.4 us -> 53.7 us (0.936)
  the two profiles are of different devices: /device:TPU:8 before, /device:TPU:24 now
where the time goes in v5:
time: 53.7 us; the launch traced here: 53.5 us
  Pallas kernels  51.5 us (96%)
  local copies, waits for them, and re-layouts  1.35 us (3%)
  between operations  0.66 us (1%)
    pallas_call x1, Pallas kernels, per_device(): pl.pallas_call(functools.partial(kernel, levels, groups), out_shape=jax.S...  51.5 us
    unnamed x1, local copies, waits for them, and re-layouts  1.35 us

profile of v5, /device:TPU:24, one launch (start us, length us, event | category | flops | bytes accessed | tf_op | source)
XLA Modules:
  0.0 53.5 jit_solution(10821050208183386679)
XLA Ops:
  0.7 51.5 %ring_attention.1 = bf16[1,4,24,128]{3,2,1,0:T(8,128)(2,1)} custom-call(bf16[1,4,24,128]{3,2,1,0:T(8,128)(2,1)} %q_hbm.1, bf16[1,4096,128]{2,1,0:T(8,128)(2,1)} %k_hbm.1, bf16[1,4096,128]{2,1,0:T(8,128)(2,1)} %v_hbm.1, s32[1]{0:T(128)S(6)} %copy.9.count_hbm, bf16[1,6,128]{2,1,0:T(8,128)(2,1)} %nk_hbm.1, bf16[1,6,128]{2,1,0:T(8,128)(2,1)} %nv_hbm.1, s32[384]{0:T(512)} %pos_hbm.1), custom_call_target="tpu_custom_call" | custom-call | flops 3221225472 | bytes 2097152 | tf_op jit(solution)/shard_map/ring_attention/pallas_call | solution.py:356
  52.2 1.3 %copy.10 = bf16[1,4,24,128]{3,2,1,0:T(8,128)(2,1)} copy(bf16[1,4,24,128]{3,2,1,0:T(8,128)(2,1)} %ring_attention.1) | data formatting | bytes 49152

commit v6 on v5

--- a/solution.py
+++ b/solution.py
@@ -20,7 +20,7 @@
 def kernel(
     levels, groups, q_hbm, k_hbm, v_hbm, count_hbm, nk_hbm, nv_hbm, pos_hbm, out_ref,
     q_ref, nk_ref, nv_ref, count_ref, pos_ref, loaded, keys, values, fresh, fresh_keys, fresh_values, wide, place_col, place_row,
-    scores_even, scores_odd, extra, tops, queries, total, peaks,
+    scores, extra, tops, queries, total, peaks,
     sent, landed,
     load_sem, fresh_send, fresh_recv, ag_send, ag_recv, back_send, back_recv,
 ):
@@ -64,15 +64,45 @@
             barrier, inc=1, device_id={"qh": lax.rem(group + k, groups)}, device_id_type=pl.DeviceIdType.MESH
         )
 
-    for load in loads[:5]:
-        load.wait()
+    loads[0].wait()
     queries[near - 1, 3 * rows:4 * rows, :] = (
         q_ref[0].astype(jnp.float32).reshape(rows, width).astype(jnp.bfloat16)
     )
+    pl.semaphore_wait(barrier, len(partners) + groups - 1)
+
+    own = queries.at[near - 1, 3 * rows:4 * rows]
+
+    def part(quarter):
+        return pl.ds(pl.multiple_of(quarter * rows, 32), rows)
+
+    def query_copy(quarter, step, src, hop):
+        return send(
+            src, queries.at[step, part(quarter)], ag_send.at[quarter, step], ag_recv.at[quarter, step],
+            {"ctx": level(hop * (1 - 2 * (quarter % 2)))},
+        )
+
+    for quarter in range(quarters):
+        query_copy(quarter, 0, own, near + 1 if quarter >= 2 else 1).start()
+
+    for load in loads[1:5]:
+        load.wait()
     wide[...] = jnp.zeros_like(wide)
     wide[0:own_new, :] = nk_ref[0].astype(jnp.float32)
     wide[STATS:STATS + own_new, :] = nv_ref[0].astype(jnp.float32)
     fresh[group] = wide[...].astype(jnp.bfloat16)
+
+    def fresh_copy(k):
+        return send(
+            fresh.at[group], fresh.at[group], fresh_send.at[k], fresh_recv.at[group],
+            {"qh": lax.rem(group + k, groups)},
+        )
+
+    def fresh_arrival(k):
+        other = lax.rem(group + k, groups)
+        return send(fresh.at[other], fresh.at[other], fresh_send.at[k], fresh_recv.at[other], {"qh": other})
+
+    for k in range(1, groups):
+        fresh_copy(k).start()
 
     def note_places(j, _):
         for i in range(tokens):
@@ -87,35 +117,6 @@
             place = pos_ref[me * tokens + g * own_new + i]
             row = jnp.where(lane == g * STATS + i, place, row)
     place_row[...] = row
-
-    pl.semaphore_wait(barrier, len(partners) + groups - 1)
-
-    own = queries.at[near - 1, 3 * rows:4 * rows]
-
-    def part(quarter):
-        return slice(quarter * rows, (quarter + 1) * rows)
-
-    def query_copy(quarter, step, src, hop):
-        return send(
-            src, queries.at[step, part(quarter)], ag_send.at[quarter, step], ag_recv.at[quarter, step],
-            {"ctx": level(hop if quarter % 2 == 0 else -hop)},
-        )
-
-    for quarter in range(quarters):
-        query_copy(quarter, 0, own, near + 1 if quarter >= 2 else 1).start()
-
-    def fresh_copy(k):
-        return send(
-            fresh.at[group], fresh.at[group], fresh_send.at[k], fresh_recv.at[group],
-            {"qh": lax.rem(group + k, groups)},
-        )
-
-    def fresh_arrival(k):
-        other = lax.rem(group + k, groups)
-        return send(fresh.at[other], fresh.at[other], fresh_send.at[k], fresh_recv.at[other], {"qh": other})
-
-    for k in range(1, groups):
-        fresh_copy(k).start()
 
     count = count_ref[0]
     loads[5].wait()
@@ -145,12 +146,10 @@
         fresh_keys[g * STATS:(g + 1) * STATS, :] = fresh[g, 0:STATS, :]
         fresh_values[g * STATS:(g + 1) * STATS, 0:width] = fresh[g, STATS:2 * STATS, :]
 
-    scores = (scores_even, scores_odd)
-
     def score_tile(step, j):
         at = pl.ds(pl.multiple_of(j * TILE, TILE), TILE)
         made = contract(queries[step], keys[:, at], ((1,), (0,)))
-        scores[step % 2][j] = made
+        scores[j] = made
         top = tops[...]
         for g in range(TILE // LANES):
             top = jnp.maximum(top, made[:, g * LANES:(g + 1) * LANES])
@@ -163,7 +162,7 @@
         made = contract(queries[step], fresh_keys[...], ((1,), (1,)))
         owners = (
             level(-(step + 1)), level(step + 1), level(-(step + near + 1)),
-            me if step == near - 1 else level(step + near + 1),
+            jnp.where(step == near - 1, me, level(step + near + 1)),
         )
 
         def causal(owner, made):
@@ -172,8 +171,8 @@
             limit = jnp.broadcast_to(place_row[0:1, :], place.shape)
             return jnp.where(limit <= place, made, -1e30)
 
-        made = jnp.concatenate([causal(owners[q], made[part(q)]) for q in range(quarters)], axis=0)
-        extra[step % 2] = made
+        made = jnp.concatenate([causal(owners[q], made[q * rows:(q + 1) * rows]) for q in range(quarters)], axis=0)
+        extra[...] = made
         top = jnp.max(jnp.maximum(tops[...], made), axis=1, keepdims=True)
         top = top.astype(jnp.bfloat16).astype(jnp.float32)
         peaks[step] = jnp.broadcast_to(top, (quarters * rows, LANES))
@@ -185,12 +184,12 @@
         ]
 
     def weigh_start(step):
-        weight = weigh(extra[step % 2], peaks[step] * factor)[0].astype(jnp.bfloat16)
+        weight = weigh(extra[...], peaks[step] * factor)[0].astype(jnp.bfloat16)
         total[step] = contract(weight, fresh_values[...], ((1,), (0,)))
 
     def weigh_tile(step, j):
         at = pl.ds(pl.multiple_of(j * TILE, TILE), TILE)
-        weight = jnp.concatenate(weigh(scores[step % 2][j], peaks[step] * factor), axis=1).astype(jnp.bfloat16)
+        weight = jnp.concatenate(weigh(scores[j], peaks[step] * factor), axis=1).astype(jnp.bfloat16)
         total[step] += contract(weight, values[at, :], ((1,), (0,)))
 
     eye = lax.broadcasted_iota(jnp.int32, (rows, LANES), 0) == lax.broadcasted_iota(jnp.int32, (rows, LANES), 1)
@@ -227,85 +226,92 @@
         wb = jnp.exp2((b[2] - peak) * factor)
         return a[0] * wa + b[0] * wb, a[1] * wa + b[1] * wb, peak
 
-    last_step = (near - 1, near - 1, near - 1, near - 2)
-    furthest = (near, near, half, half - 1)
+    def last_step(quarter):
+        return near - 1 - quarter // 3
 
     def back_copy(quarter, step):
-        hop = -furthest[quarter] if step == last_step[quarter] else 1
+        hop = jnp.where(step == last_step(quarter), -(near + near * (quarter // 2) - quarter // 3), 1)
         return send(
             sent.at[quarter, step], landed.at[quarter, step], back_send.at[quarter, step],
-            back_recv.at[quarter, step], {"ctx": level(hop if quarter % 2 == 0 else -hop)},
-        )
-
-    def pass_first(quarter):
-        pack(sent.at[quarter, 0], local(0, quarter))
-        back_copy(quarter, 0).start()
-
-    def pass_merged(quarter, step):
-        back_copy(quarter, step - 1).wait_recv()
-        pack(sent.at[quarter, step], merge(local(step, quarter), unpack(landed.at[quarter, step - 1])))
+            back_recv.at[quarter, step], {"ctx": level(hop * (1 - 2 * (quarter % 2)))},
+        )
+
+    def pass_on(quarter, step):
+        @pl.when(step > 0)
+        def _():
+            back_copy(quarter, step - 1).wait_recv()
+            number, mass, peak = merge(local(step, quarter), unpack(landed.at[quarter, step - 1]))
+            total[step, part(quarter), 0:width] = number
+            total[step, part(quarter), width:2 * width] = mass
+            peaks[step, part(quarter), :] = peak
+
+        pack(sent.at[quarter, step], local(step, quarter))
         back_copy(quarter, step).start()
 
-    def arrive(quarter, step):
-        query_copy(quarter, step, own, 1).wait_recv()
-
-    def follow(quarter, step):
-        query_copy(quarter, step + 1, queries.at[step, part(quarter)], 1).start()
+    def every(count, body):
+        lax.fori_loop(0, count, lambda i, _: (body(i), 0)[1], 0)
 
     def forward(step):
-        for quarter in range(quarters):
-            if step <= last_step[quarter]:
-                arrive(quarter, step)
-            if step < last_step[quarter]:
-                follow(quarter, step)
+        def one(quarter):
+            @pl.when(step <= last_step(quarter))
+            def _():
+                query_copy(quarter, step, own, 1).wait_recv()
+
+            @pl.when(step < last_step(quarter))
+            def _():
+                query_copy(quarter, step + 1, queries.at[step, part(quarter)], 1).start()
+
+        every(quarters, one)
 
     forward(0)
     score_start()
-
-    def first(j, _):
-        score_tile(0, j)
-        return 0
-
-    lax.fori_loop(0, tiles, first, 0)
+    every(tiles, lambda j: score_tile(0, j))
     score_end(0)
 
-    for step in range(near - 1):
-        forward(step + 1)
-        score_start()
+    def turn(step):
         weigh_start(step)
 
-        def both(j, _):
-            score_tile(step + 1, j)
-            weigh_tile(step, j)
-            return 0
-
-        lax.fori_loop(0, tiles, both, 0)
-        score_end(step + 1)
-        for quarter in range(quarters):
-            if step == 0:
-                pass_first(quarter)
-            else:
-                pass_merged(quarter, step)
-
-    weigh_start(near - 1)
-
-    def last(j, _):
-        weigh_tile(near - 1, j)
-        return 0
-
-    lax.fori_loop(0, tiles, last, 0)
-    for quarter in (2, 0, 1):
-        pass_merged(quarter, near - 1)
+        @pl.when(step < near - 1)
+        def _():
+            forward(step + 1)
+            score_start()
+
+            def both(j):
+                weigh_tile(step, j)
+                score_tile(step + 1, j)
+
+            every(tiles, both)
+            score_end(step + 1)
+
+        @pl.when(step == near - 1)
+        def _():
+            every(tiles, lambda j: weigh_tile(step, j))
+
+        def one(i):
+            quarter = quarters - 1 - i
+
+            @pl.when(step <= last_step(quarter))
+            def _():
+                pass_on(quarter, step)
+
+        every(quarters, one)
+
+    every(near, turn)
     result = local(near - 1, 3)
     for quarter in (3, 0, 1, 2):
-        back_copy(quarter, last_step[quarter]).wait_recv()
-        result = merge(result, unpack(landed.at[quarter, last_step[quarter]]))
+        back_copy(quarter, last_step(quarter)).wait_recv()
+        result = merge(result, unpack(landed.at[quarter, last_step(quarter)]))
     out_ref[0] = (result[0] / result[1]).reshape(heads, tokens, width).astype(jnp.bfloat16)
 
-    for quarter in range(quarters):
-        for step in range(last_step[quarter] + 1):
+    def finish(i):
+        quarter, step = i // near, i % near
+
+        @pl.when(step <= last_step(quarter))
+        def _():
             query_copy(quarter, step, own, 1).wait_send()
             back_copy(quarter, step).wait_send()
+
+    every(quarters * near, finish)
     for k in range(1, groups):
         fresh_copy(k).wait_send()
 
@@ -337,8 +343,7 @@
         pltpu.VMEM((levels * tokens, LANES), jnp.int32),
         pltpu.VMEM((8, LANES), jnp.int32),
         pltpu.VMEM((slots // TILE, 4 * rows, TILE), jnp.float32),
-        pltpu.VMEM((slots // TILE, 4 * rows, TILE), jnp.float32),
-        pltpu.VMEM((2, 4 * rows, LANES), jnp.float32),
+        pltpu.VMEM((4 * rows, LANES), jnp.float32),
         pltpu.VMEM((4 * rows, LANES), jnp.float32),
         pltpu.VMEM((near, 4 * rows, width), jnp.bfloat16),
         pltpu.VMEM((near, 4 * rows, 2 * width), jnp.float32),

time: 53.7 us -> 54 us (level)
  the two profiles are of different devices: /device:TPU:24 before, /device:TPU:6 now
where the time goes in v6:
time: 54 us; the launch traced here: 53.8 us
  Pallas kernels  51.7 us (96%)
  local copies, waits for them, and re-layouts  1.35 us (2%)
  between operations  0.66 us (1%)
    pallas_call x1, Pallas kernels, per_device(): pl.pallas_call(functools.partial(kernel, levels, groups), out_shape=jax.S...  51.7 us
    unnamed x1, local copies, waits for them, and re-layouts  1.35 us

profile of v6, /device:TPU:6, one launch (start us, length us, event | category | flops | bytes accessed | tf_op | source)
XLA Modules:
  0.0 53.8 jit_solution(15371934590459311157)
XLA Ops:
  0.7 51.7 %ring_attention.1 = bf16[1,4,24,128]{3,2,1,0:T(8,128)(2,1)} custom-call(bf16[1,4,24,128]{3,2,1,0:T(8,128)(2,1)} %q_hbm.1, bf16[1,4096,128]{2,1,0:T(8,128)(2,1)} %k_hbm.1, bf16[1,4096,128]{2,1,0:T(8,128)(2,1)} %v_hbm.1, s32[1]{0:T(128)S(6)} %copy.9.count_hbm, bf16[1,6,128]{2,1,0:T(8,128)(2,1)} %nk_hbm.1, bf16[1,6,128]{2,1,0:T(8,128)(2,1)} %nv_hbm.1, s32[384]{0:T(512)} %pos_hbm.1), custom_call_target="tpu_custom_call" | custom-call | flops 3221225472 | bytes 2097152 | tf_op jit(solution)/shard_map/ring_attention/pallas_call | solution.py:361
  52.4 1.3 %copy.10 = bf16[1,4,24,128]{3,2,1,0:T(8,128)(2,1)} copy(bf16[1,4,24,128]{3,2,1,0:T(8,128)(2,1)} %ring_attention.1) | data formatting | bytes 49152

commit v7 on v6

--- a/solution.py
+++ b/solution.py
@@ -8,7 +8,7 @@
 from jax.sharding import PartitionSpec as P
 
 LOG2E = 1.4426950408889634
-TILE = 1024
+TILE = 2048
 LANES = 128
 STATS = 16
 
@@ -30,7 +30,7 @@
     tiles = slots // TILE
     half = levels // 2
     near = half // 2
-    quarters = 4
+    sides = 2
     own_new = nk_ref.shape[1]
     factor = LOG2E * width ** -0.5
     me = lax.axis_index("ctx")
@@ -56,7 +56,7 @@
         load.start()
 
     barrier = pltpu.get_barrier_semaphore()
-    partners = (1, -1, near + 1, -near - 1, near, -near, half - 1, 1 - half, half)
+    partners = (1, -1, near + 1, -near - 1)
     for distance in partners:
         pl.semaphore_signal(barrier, inc=1, device_id={"ctx": level(distance)}, device_id_type=pl.DeviceIdType.MESH)
     for k in range(1, groups):
@@ -65,24 +65,24 @@
         )
 
     loads[0].wait()
-    queries[near - 1, 3 * rows:4 * rows, :] = (
+    queries[half - 1, rows:2 * rows, :] = (
         q_ref[0].astype(jnp.float32).reshape(rows, width).astype(jnp.bfloat16)
     )
     pl.semaphore_wait(barrier, len(partners) + groups - 1)
 
-    own = queries.at[near - 1, 3 * rows:4 * rows]
-
-    def part(quarter):
-        return pl.ds(pl.multiple_of(quarter * rows, 32), rows)
-
-    def query_copy(quarter, step, src, hop):
+    own = queries.at[half - 1, rows:2 * rows]
+
+    def part(side):
+        return pl.ds(pl.multiple_of(side * rows, 32), rows)
+
+    def query_copy(side, step, src):
         return send(
-            src, queries.at[step, part(quarter)], ag_send.at[quarter, step], ag_recv.at[quarter, step],
-            {"ctx": level(hop * (1 - 2 * (quarter % 2)))},
-        )
-
-    for quarter in range(quarters):
-        query_copy(quarter, 0, own, near + 1 if quarter >= 2 else 1).start()
+            src, queries.at[step, part(side)], ag_send.at[side, step], ag_recv.at[side, step],
+            {"ctx": level(1 - 2 * side)},
+        )
+
+    for side in range(sides):
+        query_copy(side, 0, own).start()
 
     for load in loads[1:5]:
         load.wait()
@@ -160,10 +160,7 @@
 
     def score_end(step):
         made = contract(queries[step], fresh_keys[...], ((1,), (1,)))
-        owners = (
-            level(-(step + 1)), level(step + 1), level(-(step + near + 1)),
-            jnp.where(step == near - 1, me, level(step + near + 1)),
-        )
+        owners = (level(-(step + 1)), jnp.where(step == half - 1, me, level(step + 1)))
 
         def causal(owner, made):
             place = place_col[pl.ds(pl.multiple_of(owner * tokens, 8), tokens), :]
@@ -171,11 +168,11 @@
             limit = jnp.broadcast_to(place_row[0:1, :], place.shape)
             return jnp.where(limit <= place, made, -1e30)
 
-        made = jnp.concatenate([causal(owners[q], made[q * rows:(q + 1) * rows]) for q in range(quarters)], axis=0)
+        made = jnp.concatenate([causal(owners[i], made[i * rows:(i + 1) * rows]) for i in range(sides)], axis=0)
         extra[...] = made
         top = jnp.max(jnp.maximum(tops[...], made), axis=1, keepdims=True)
         top = top.astype(jnp.bfloat16).astype(jnp.float32)
-        peaks[step] = jnp.broadcast_to(top, (quarters * rows, LANES))
+        peaks[step] = jnp.broadcast_to(top, (sides * rows, LANES))
 
     def weigh(made, peak):
         return [
@@ -216,8 +213,8 @@
 
         return number, column(stats[1:2, :] + stats[2:3, :]), column(stats[0:1, :])
 
-    def local(step, quarter):
-        at = part(quarter)
+    def local(step, side):
+        at = part(side)
         return total[step, at, 0:width], total[step, at, width:2 * width], peaks[step, at, :]
 
     def merge(a, b):
@@ -226,42 +223,39 @@
         wb = jnp.exp2((b[2] - peak) * factor)
         return a[0] * wa + b[0] * wb, a[1] * wa + b[1] * wb, peak
 
-    def last_step(quarter):
-        return near - 1 - quarter // 3
-
-    def back_copy(quarter, step):
-        hop = jnp.where(step == last_step(quarter), -(near + near * (quarter // 2) - quarter // 3), 1)
+    def back_copy(side, step):
+        hop = jnp.where(step == near, near + 1, 1)
         return send(
-            sent.at[quarter, step], landed.at[quarter, step], back_send.at[quarter, step],
-            back_recv.at[quarter, step], {"ctx": level(hop * (1 - 2 * (quarter % 2)))},
-        )
-
-    def pass_on(quarter, step):
-        @pl.when(step > 0)
-        def _():
-            back_copy(quarter, step - 1).wait_recv()
-            number, mass, peak = merge(local(step, quarter), unpack(landed.at[quarter, step - 1]))
-            total[step, part(quarter), 0:width] = number
-            total[step, part(quarter), width:2 * width] = mass
-            peaks[step, part(quarter), :] = peak
-
-        pack(sent.at[quarter, step], local(step, quarter))
-        back_copy(quarter, step).start()
+            sent.at[side, step], landed.at[side, step], back_send.at[side, step], back_recv.at[side, step],
+            {"ctx": level(hop * (2 * side - 1))},
+        )
+
+    def pass_on(side, step, merged):
+        @pl.when(merged)
+        def _():
+            back_copy(side, step + 1).wait_recv()
+            number, mass, peak = merge(local(step, side), unpack(landed.at[side, step + 1]))
+            total[step, part(side), 0:width] = number
+            total[step, part(side), width:2 * width] = mass
+            peaks[step, part(side), :] = peak
+
+        pack(sent.at[side, step], local(step, side))
+        back_copy(side, step).start()
 
     def every(count, body):
         lax.fori_loop(0, count, lambda i, _: (body(i), 0)[1], 0)
 
     def forward(step):
-        def one(quarter):
-            @pl.when(step <= last_step(quarter))
+        def one(side):
+            @pl.when(step + side < half)
             def _():
-                query_copy(quarter, step, own, 1).wait_recv()
-
-            @pl.when(step < last_step(quarter))
+                query_copy(side, step, own).wait_recv()
+
+            @pl.when(step + side < half - 1)
             def _():
-                query_copy(quarter, step + 1, queries.at[step, part(quarter)], 1).start()
-
-        every(quarters, one)
+                query_copy(side, step + 1, queries.at[step, part(side)]).start()
+
+        every(sides, one)
 
     forward(0)
     score_start()
@@ -271,7 +265,7 @@
     def turn(step):
         weigh_start(step)
 
-        @pl.when(step < near - 1)
+        @pl.when(step < half - 1)
         def _():
             forward(step + 1)
             score_start()
@@ -283,35 +277,36 @@
             every(tiles, both)
             score_end(step + 1)
 
-        @pl.when(step == near - 1)
+        @pl.when(step == half - 1)
         def _():
             every(tiles, lambda j: weigh_tile(step, j))
 
-        def one(i):
-            quarter = quarters - 1 - i
-
-            @pl.when(step <= last_step(quarter))
-            def _():
-                pass_on(quarter, step)
-
-        every(quarters, one)
-
-    every(near, turn)
-    result = local(near - 1, 3)
-    for quarter in (3, 0, 1, 2):
-        back_copy(quarter, last_step(quarter)).wait_recv()
-        result = merge(result, unpack(landed.at[quarter, last_step(quarter)]))
+        @pl.when(step >= half - 2)
+        def _():
+            pass_on(half - 1 - step, step, step < 0)
+
+        @pl.when((step >= near - 1) & (step < half - 1))
+        def _():
+            every(sides, lambda side: pass_on(side, jnp.where(step < near, step, half - 2 - step), step >= near))
+
+    every(half, turn)
+    for side, step in ((1, half - 3), (0, half - 2), (1, half - 4), (0, half - 3), (0, half - 4)):
+        pass_on(side, step, step >= 0)
+    result = local(half - 1, 1)
+    for side, step in ((0, 0), (1, 0), (1, near), (0, near)):
+        back_copy(side, step).wait_recv()
+        result = merge(result, unpack(landed.at[side, step]))
     out_ref[0] = (result[0] / result[1]).reshape(heads, tokens, width).astype(jnp.bfloat16)
 
     def finish(i):
-        quarter, step = i // near, i % near
-
-        @pl.when(step <= last_step(quarter))
-        def _():
-            query_copy(quarter, step, own, 1).wait_send()
-            back_copy(quarter, step).wait_send()
-
-    every(quarters * near, finish)
+        side, step = i // half, i % half
+
+        @pl.when(step + side < half)
+        def _():
+            query_copy(side, step, own).wait_send()
+            back_copy(side, step).wait_send()
+
+    every(sides * half, finish)
     for k in range(1, groups):
         fresh_copy(k).wait_send()
 
@@ -322,7 +317,7 @@
     _, heads, tokens, width = queries.shape
     slots = cache_keys.shape[1]
     rows = heads * tokens
-    near = levels // 4
+    half = levels // 2
     vmem = pl.BlockSpec(memory_space=pltpu.VMEM)
     anywhere = pl.BlockSpec(memory_space=pl.ANY)
     packed = rows + STATS
@@ -342,21 +337,21 @@
         pltpu.VMEM((2 * STATS, width), jnp.float32),
         pltpu.VMEM((levels * tokens, LANES), jnp.int32),
         pltpu.VMEM((8, LANES), jnp.int32),
-        pltpu.VMEM((slots // TILE, 4 * rows, TILE), jnp.float32),
-        pltpu.VMEM((4 * rows, LANES), jnp.float32),
-        pltpu.VMEM((4 * rows, LANES), jnp.float32),
-        pltpu.VMEM((near, 4 * rows, width), jnp.bfloat16),
-        pltpu.VMEM((near, 4 * rows, 2 * width), jnp.float32),
-        pltpu.VMEM((near, 4 * rows, LANES), jnp.float32),
-        pltpu.VMEM((4, near, packed, width), jnp.bfloat16),
-        pltpu.VMEM((4, near, packed, width), jnp.bfloat16),
+        pltpu.VMEM((slots // TILE, 2 * rows, TILE), jnp.float32),
+        pltpu.VMEM((2 * rows, LANES), jnp.float32),
+        pltpu.VMEM((2 * rows, LANES), jnp.float32),
+        pltpu.VMEM((half, 2 * rows, width), jnp.bfloat16),
+        pltpu.VMEM((half, 2 * rows, 2 * width), jnp.float32),
+        pltpu.VMEM((half, 2 * rows, LANES), jnp.float32),
+        pltpu.VMEM((2, half, packed, width), jnp.bfloat16),
+        pltpu.VMEM((2, half, packed, width), jnp.bfloat16),
         dma((7,)),
         dma((groups,)),
         dma((groups,)),
-        dma((4, near)),
-        dma((4, near)),
-        dma((4, near)),
-        dma((4, near)),
+        dma((2, half)),
+        dma((2, half)),
+        dma((2, half)),
+        dma((2, half)),
     ]
     return pl.pallas_call(
         functools.partial(kernel, levels, groups),

time: 54 us -> 63 us (1.17)
  the two profiles are of different devices: /device:TPU:6 before, /device:TPU:24 now
where the time goes in v7:
time: 63 us; the launch traced here: 62.8 us
  Pallas kernels  60.8 us (97%)
  local copies, waits for them, and re-layouts  1.35 us (2%)
  between operations  0.66 us (1%)
    pallas_call x1, Pallas kernels, per_device(): pl.pallas_call(functools.partial(kernel, levels, groups), out_shape=jax.S...  60.8 us
    unnamed x1, local copies, waits for them, and re-layouts  1.35 us

profile of v7, /device:TPU:24, one launch (start us, length us, event | category | flops | bytes accessed | tf_op | source)
XLA Modules:
  0.0 62.8 jit_solution(2912358858550653101)
XLA Ops:
  0.7 60.8 %ring_attention.1 = bf16[1,4,24,128]{3,2,1,0:T(8,128)(2,1)} custom-call(bf16[1,4,24,128]{3,2,1,0:T(8,128)(2,1)} %q_hbm.1, bf16[1,4096,128]{2,1,0:T(8,128)(2,1)} %k_hbm.1, bf16[1,4096,128]{2,1,0:T(8,128)(2,1)} %v_hbm.1, s32[1]{0:T(128)S(6)} %copy.9.count_hbm, bf16[1,6,128]{2,1,0:T(8,128)(2,1)} %nk_hbm.1, bf16[1,6,128]{2,1,0:T(8,128)(2,1)} %nv_hbm.1, s32[384]{0:T(512)} %pos_hbm.1), custom_call_target="tpu_custom_call" | custom-call | flops 3221225472 | bytes 2097152 | tf_op jit(solution)/shard_map/ring_attention/pallas_call | solution.py:356
  61.5 1.3 %copy.10 = bf16[1,4,24,128]{3,2,1,0:T(8,128)(2,1)} copy(bf16[1,4,24,128]{3,2,1,0:T(8,128)(2,1)} %ring_attention.1) | data formatting | bytes 49152

commit v8 on v6

--- a/solution.py
+++ b/solution.py
@@ -192,29 +192,26 @@
         weight = jnp.concatenate(weigh(scores[j], peaks[step] * factor), axis=1).astype(jnp.bfloat16)
         total[step] += contract(weight, values[at, :], ((1,), (0,)))
 
-    eye = lax.broadcasted_iota(jnp.int32, (rows, LANES), 0) == lax.broadcasted_iota(jnp.int32, (rows, LANES), 1)
+    lanes = lax.broadcasted_iota(jnp.int32, (rows, LANES), 1)
+    line = lax.broadcasted_iota(jnp.int32, (STATS, LANES), 0)
+    pick = jnp.where(line == lax.broadcasted_iota(jnp.int32, (STATS, LANES), 1), 1.0, 0.0).astype(jnp.bfloat16)
+    spread = jnp.concatenate(
+        [jnp.where(line == 0, 1.0, 0.0), jnp.where((line == 1) | (line == 2), 1.0, 0.0)], axis=1
+    ).astype(jnp.bfloat16)
 
     def pack(ref, summed):
         number, mass, peak = summed
         ref[0:rows, :] = number.astype(jnp.bfloat16)
-        peak_row = jnp.sum(jnp.where(eye, peak, 0.0), axis=0, keepdims=True)
-        mass_row = jnp.sum(jnp.where(eye, mass, 0.0), axis=0, keepdims=True)
-        mass_high = mass_row.astype(jnp.bfloat16).astype(jnp.float32)
-        line = lax.broadcasted_iota(jnp.int32, (STATS, LANES), 0)
-        stats = jnp.where(
-            line == 0, peak_row, jnp.where(line == 1, mass_high, jnp.where(line == 2, mass_row - mass_high, 0.0))
-        )
-        ref[rows:rows + STATS, :] = stats.astype(jnp.bfloat16)
+        mass_high = mass.astype(jnp.bfloat16).astype(jnp.float32)
+        column = jnp.where(
+            lanes == 0, peak, jnp.where(lanes == 1, mass_high, jnp.where(lanes == 2, mass - mass_high, 0.0))
+        )
+        column = jnp.concatenate([column, jnp.zeros((LANES - rows, LANES), jnp.float32)], axis=0)
+        ref[rows:rows + STATS, :] = contract(pick, column.astype(jnp.bfloat16), ((1,), (1,))).astype(jnp.bfloat16)
 
     def unpack(ref):
-        number = ref[0:rows, :].astype(jnp.float32)
-        stats = ref[rows:rows + STATS, :].astype(jnp.float32)
-
-        def column(line):
-            spread = jnp.where(eye, jnp.broadcast_to(line, (rows, LANES)), 0.0)
-            return jnp.broadcast_to(jnp.sum(spread, axis=1, keepdims=True), (rows, LANES))
-
-        return number, column(stats[1:2, :] + stats[2:3, :]), column(stats[0:1, :])
+        both = contract(ref[rows:rows + STATS, :], spread, ((0,), (0,)))[0:rows]
+        return ref[0:rows, :].astype(jnp.float32), both[:, width:2 * width], both[:, 0:width]
 
     def local(step, quarter):
         at = part(quarter)
@@ -236,17 +233,17 @@
             back_recv.at[quarter, step], {"ctx": level(hop * (1 - 2 * (quarter % 2)))},
         )
 
-    def pass_on(quarter, step):
-        @pl.when(step > 0)
-        def _():
-            back_copy(quarter, step - 1).wait_recv()
-            number, mass, peak = merge(local(step, quarter), unpack(landed.at[quarter, step - 1]))
-            total[step, part(quarter), 0:width] = number
-            total[step, part(quarter), width:2 * width] = mass
-            peaks[step, part(quarter), :] = peak
-
-        pack(sent.at[quarter, step], local(step, quarter))
-        back_copy(quarter, step).start()
+    def pass_on(step, chosen, merged):
+        if merged:
+            for quarter in chosen:
+                back_copy(quarter, step - 1).wait_recv()
+        for quarter in chosen:
+            summed = local(step, quarter)
+            if merged:
+                summed = merge(summed, unpack(landed.at[quarter, step - 1]))
+            pack(sent.at[quarter, step], summed)
+        for quarter in chosen:
+            back_copy(quarter, step).start()
 
     def every(count, body):
         lax.fori_loop(0, count, lambda i, _: (body(i), 0)[1], 0)
@@ -287,20 +284,21 @@
         def _():
             every(tiles, lambda j: weigh_tile(step, j))
 
-        def one(i):
-            quarter = quarters - 1 - i
-
-            @pl.when(step <= last_step(quarter))
-            def _():
-                pass_on(quarter, step)
-
-        every(quarters, one)
+        everyone = (2, 3, 0, 1)
+        pl.when(step == 0)(lambda: pass_on(step, everyone, False))
+        pl.when((step > 0) & (step < near - 1))(lambda: pass_on(step, everyone, True))
 
     every(near, turn)
-    result = local(near - 1, 3)
+    pass_on(near - 1, (2, 0, 1), True)
     for quarter in (3, 0, 1, 2):
         back_copy(quarter, last_step(quarter)).wait_recv()
-        result = merge(result, unpack(landed.at[quarter, last_step(quarter)]))
+    gathered = [local(near - 1, 3)] + [unpack(landed.at[quarter, last_step(quarter)]) for quarter in range(quarters)]
+    peak = functools.reduce(jnp.maximum, [one[2] for one in gathered])
+    shares = [jnp.exp2((one[2] - peak) * factor) for one in gathered]
+    result = (
+        sum(one[0] * share for one, share in zip(gathered, shares)),
+        sum(one[1] * share for one, share in zip(gathered, shares)),
+    )
     out_ref[0] = (result[0] / result[1]).reshape(heads, tokens, width).astype(jnp.bfloat16)
 
     def finish(i):

time: 54 us -> 56.4 us (1.044)
  the two profiles are of different devices: /device:TPU:6 before, /device:TPU:12 now
where the time goes in v8:
time: 56.4 us; the launch traced here: 56.2 us
  Pallas kernels  54.2 us (96%)
  local copies, waits for them, and re-layouts  1.35 us (2%)
  between operations  0.66 us (1%)
    pallas_call x1, Pallas kernels, per_device(): pl.pallas_call(functools.partial(kernel, levels, groups), out_shape=jax.S...  54.2 us
    unnamed x1, local copies, waits for them, and re-layouts  1.35 us

profile of v8, /device:TPU:12, one launch (start us, length us, event | category | flops | bytes accessed | tf_op | source)
XLA Modules:
  0.0 56.2 jit_solution(15019371217337936809)
XLA Ops:
  0.7 54.2 %ring_attention.1 = bf16[1,4,24,128]{3,2,1,0:T(8,128)(2,1)} custom-call(bf16[1,4,24,128]{3,2,1,0:T(8,128)(2,1)} %q_hbm.1, bf16[1,4096,128]{2,1,0:T(8,128)(2,1)} %k_hbm.1, bf16[1,4096,128]{2,1,0:T(8,128)(2,1)} %v_hbm.1, s32[1]{0:T(128)S(6)} %copy.9.count_hbm, bf16[1,6,128]{2,1,0:T(8,128)(2,1)} %nk_hbm.1, bf16[1,6,128]{2,1,0:T(8,128)(2,1)} %nv_hbm.1, s32[384]{0:T(512)} %pos_hbm.1), custom_call_target="tpu_custom_call" | custom-call | flops 3221225472 | bytes 2097152 | tf_op jit(solution)/shard_map/ring_attention/pallas_call | solution.py:359
  54.9 1.3 %copy.10 = bf16[1,4,24,128]{3,2,1,0:T(8,128)(2,1)} copy(bf16[1,4,24,128]{3,2,1,0:T(8,128)(2,1)} %ring_attention.1) | data formatting | bytes 49152

commit v9 on v6

--- a/solution.py
+++ b/solution.py
@@ -30,7 +30,16 @@
     tiles = slots // TILE
     half = levels // 2
     near = half // 2
-    quarters = 4
+    members = ((0, 1, 4), (0, 1, 2)) + ((0, 1, 2, 3),) * (near - 2) + ((2, 3),)
+    steps = len(members)
+    streams = (0, 1, 2, 3)
+    first_step = (0, 0, 1, 2)
+    last_step = (near - 1, near - 1, near, near)
+    sign = (1, -1, 1, -1)
+
+    def distance(stream, step):
+        return step + 1 if stream < 2 else half + 1 - step
+
     own_new = nk_ref.shape[1]
     factor = LOG2E * width ** -0.5
     me = lax.axis_index("ctx")
@@ -57,32 +66,38 @@
 
     barrier = pltpu.get_barrier_semaphore()
     partners = (1, -1, near + 1, -near - 1, near, -near, half - 1, 1 - half, half)
-    for distance in partners:
-        pl.semaphore_signal(barrier, inc=1, device_id={"ctx": level(distance)}, device_id_type=pl.DeviceIdType.MESH)
+    for hop in partners:
+        pl.semaphore_signal(barrier, inc=1, device_id={"ctx": level(hop)}, device_id_type=pl.DeviceIdType.MESH)
     for k in range(1, groups):
         pl.semaphore_signal(
             barrier, inc=1, device_id={"qh": lax.rem(group + k, groups)}, device_id_type=pl.DeviceIdType.MESH
         )
 
     loads[0].wait()
-    queries[near - 1, 3 * rows:4 * rows, :] = (
+    queries[0, 2 * rows:3 * rows, :] = (
         q_ref[0].astype(jnp.float32).reshape(rows, width).astype(jnp.bfloat16)
     )
     pl.semaphore_wait(barrier, len(partners) + groups - 1)
 
-    own = queries.at[near - 1, 3 * rows:4 * rows]
-
-    def part(quarter):
-        return pl.ds(pl.multiple_of(quarter * rows, 32), rows)
-
-    def query_copy(quarter, step, src, hop):
+    own = queries.at[0, 2 * rows:3 * rows]
+
+    def part(stream, step):
+        at = members[step].index(stream)
+        return slice(at * rows, (at + 1) * rows)
+
+    def onward(stream):
+        return sign[stream] if stream < 2 else -sign[stream]
+
+    def query_copy(stream, step, src):
+        enters = step == first_step[stream]
+        hop = sign[stream] * distance(stream, step) if enters else onward(stream)
         return send(
-            src, queries.at[step, part(quarter)], ag_send.at[quarter, step], ag_recv.at[quarter, step],
-            {"ctx": level(hop * (1 - 2 * (quarter % 2)))},
-        )
-
-    for quarter in range(quarters):
-        query_copy(quarter, 0, own, near + 1 if quarter >= 2 else 1).start()
+            src, queries.at[step, part(stream, step)], ag_send.at[stream, step], ag_recv.at[stream, step],
+            {"ctx": level(hop)},
+        )
+
+    for stream in streams:
+        query_copy(stream, first_step[stream], own).start()
 
     for load in loads[1:5]:
         load.wait()
@@ -146,36 +161,39 @@
         fresh_keys[g * STATS:(g + 1) * STATS, :] = fresh[g, 0:STATS, :]
         fresh_values[g * STATS:(g + 1) * STATS, 0:width] = fresh[g, STATS:2 * STATS, :]
 
+    def height(step):
+        return len(members[step]) * rows
+
     def score_tile(step, j):
         at = pl.ds(pl.multiple_of(j * TILE, TILE), TILE)
-        made = contract(queries[step], keys[:, at], ((1,), (0,)))
-        scores[j] = made
-        top = tops[...]
+        here = slice(0, height(step))
+        made = contract(queries[step, here], keys[:, at], ((1,), (0,)))
+        scores[j, here] = made
+        top = tops[here]
         for g in range(TILE // LANES):
             top = jnp.maximum(top, made[:, g * LANES:(g + 1) * LANES])
-        tops[...] = top
+        tops[here] = top
 
     def score_start():
         tops[...] = jnp.full(tops.shape, -1e30, jnp.float32)
 
     def score_end(step):
-        made = contract(queries[step], fresh_keys[...], ((1,), (1,)))
-        owners = (
-            level(-(step + 1)), level(step + 1), level(-(step + near + 1)),
-            jnp.where(step == near - 1, me, level(step + near + 1)),
-        )
-
-        def causal(owner, made):
+        here = slice(0, height(step))
+        made = contract(queries[step, here], fresh_keys[...], ((1,), (1,)))
+
+        def causal(stream):
+            owner = me if stream == 4 else level(-sign[stream] * distance(stream, step))
+            scored = made[part(stream, step)]
             place = place_col[pl.ds(pl.multiple_of(owner * tokens, 8), tokens), :]
             place = jnp.concatenate([place] * heads, axis=0)
             limit = jnp.broadcast_to(place_row[0:1, :], place.shape)
-            return jnp.where(limit <= place, made, -1e30)
-
-        made = jnp.concatenate([causal(owners[q], made[q * rows:(q + 1) * rows]) for q in range(quarters)], axis=0)
-        extra[...] = made
-        top = jnp.max(jnp.maximum(tops[...], made), axis=1, keepdims=True)
+            return jnp.where(limit <= place, scored, -1e30)
+
+        masked = jnp.concatenate([causal(stream) for stream in members[step]], axis=0)
+        extra[here] = masked
+        top = jnp.max(jnp.maximum(tops[here], masked), axis=1, keepdims=True)
         top = top.astype(jnp.bfloat16).astype(jnp.float32)
-        peaks[step] = jnp.broadcast_to(top, (quarters * rows, LANES))
+        peaks[step, here] = jnp.broadcast_to(top, (height(step), LANES))
 
     def weigh(made, peak):
         return [
@@ -184,13 +202,15 @@
         ]
 
     def weigh_start(step):
-        weight = weigh(extra[...], peaks[step] * factor)[0].astype(jnp.bfloat16)
-        total[step] = contract(weight, fresh_values[...], ((1,), (0,)))
+        here = slice(0, height(step))
+        weight = weigh(extra[here], peaks[step, here] * factor)[0].astype(jnp.bfloat16)
+        total[step, here] = contract(weight, fresh_values[...], ((1,), (0,)))
 
     def weigh_tile(step, j):
         at = pl.ds(pl.multiple_of(j * TILE, TILE), TILE)
-        weight = jnp.concatenate(weigh(scores[j], peaks[step] * factor), axis=1).astype(jnp.bfloat16)
-        total[step] += contract(weight, values[at, :], ((1,), (0,)))
+        here = slice(0, height(step))
+        weight = jnp.concatenate(weigh(scores[j, here], peaks[step, here] * factor), axis=1).astype(jnp.bfloat16)
+        total[step, here] += contract(weight, values[at, :], ((1,), (0,)))
 
     eye = lax.broadcasted_iota(jnp.int32, (rows, LANES), 0) == lax.broadcasted_iota(jnp.int32, (rows, LANES), 1)
 
@@ -216,8 +236,8 @@
 
         return number, column(stats[1:2, :] + stats[2:3, :]), column(stats[0:1, :])
 
-    def local(step, quarter):
-        at = part(quarter)
+    def local(step, stream):
+        at = part(stream, step)
         return total[step, at, 0:width], total[step, at, width:2 * width], peaks[step, at, :]
 
     def merge(a, b):
@@ -226,53 +246,38 @@
         wb = jnp.exp2((b[2] - peak) * factor)
         return a[0] * wa + b[0] * wb, a[1] * wa + b[1] * wb, peak
 
-    def last_step(quarter):
-        return near - 1 - quarter // 3
-
-    def back_copy(quarter, step):
-        hop = jnp.where(step == last_step(quarter), -(near + near * (quarter // 2) - quarter // 3), 1)
+    def back_copy(stream, step):
+        hop = -sign[stream] * distance(stream, step) if step == last_step[stream] else onward(stream)
         return send(
-            sent.at[quarter, step], landed.at[quarter, step], back_send.at[quarter, step],
-            back_recv.at[quarter, step], {"ctx": level(hop * (1 - 2 * (quarter % 2)))},
-        )
-
-    def pass_on(quarter, step):
-        @pl.when(step > 0)
-        def _():
-            back_copy(quarter, step - 1).wait_recv()
-            number, mass, peak = merge(local(step, quarter), unpack(landed.at[quarter, step - 1]))
-            total[step, part(quarter), 0:width] = number
-            total[step, part(quarter), width:2 * width] = mass
-            peaks[step, part(quarter), :] = peak
-
-        pack(sent.at[quarter, step], local(step, quarter))
-        back_copy(quarter, step).start()
+            sent.at[stream, step], landed.at[stream, step], back_send.at[stream, step], back_recv.at[stream, step],
+            {"ctx": level(hop)},
+        )
+
+    def pass_on(stream, step):
+        summed = local(step, stream)
+        if step > first_step[stream]:
+            back_copy(stream, step - 1).wait_recv()
+            summed = merge(summed, unpack(landed.at[stream, step - 1]))
+        pack(sent.at[stream, step], summed)
+        back_copy(stream, step).start()
 
     def every(count, body):
         lax.fori_loop(0, count, lambda i, _: (body(i), 0)[1], 0)
 
     def forward(step):
-        def one(quarter):
-            @pl.when(step <= last_step(quarter))
-            def _():
-                query_copy(quarter, step, own, 1).wait_recv()
-
-            @pl.when(step < last_step(quarter))
-            def _():
-                query_copy(quarter, step + 1, queries.at[step, part(quarter)], 1).start()
-
-        every(quarters, one)
+        for stream in members[step]:
+            if stream in streams:
+                query_copy(stream, step, own).wait_recv()
+                if step < last_step[stream]:
+                    query_copy(stream, step + 1, queries.at[step, part(stream, step)]).start()
 
     forward(0)
     score_start()
     every(tiles, lambda j: score_tile(0, j))
     score_end(0)
-
-    def turn(step):
+    for step in range(steps):
         weigh_start(step)
-
-        @pl.when(step < near - 1)
-        def _():
+        if step < steps - 1:
             forward(step + 1)
             score_start()
 
@@ -282,36 +287,22 @@
 
             every(tiles, both)
             score_end(step + 1)
-
-        @pl.when(step == near - 1)
-        def _():
+        else:
             every(tiles, lambda j: weigh_tile(step, j))
-
-        def one(i):
-            quarter = quarters - 1 - i
-
-            @pl.when(step <= last_step(quarter))
-            def _():
-                pass_on(quarter, step)
-
-        every(quarters, one)
-
-    every(near, turn)
-    result = local(near - 1, 3)
-    for quarter in (3, 0, 1, 2):
-        back_copy(quarter, last_step(quarter)).wait_recv()
-        result = merge(result, unpack(landed.at[quarter, last_step(quarter)]))
+        for stream in reversed(members[step]):
+            if stream in streams:
+                pass_on(stream, step)
+
+    result = local(0, 4)
+    for stream in streams:
+        back_copy(stream, last_step[stream]).wait_recv()
+        result = merge(result, unpack(landed.at[stream, last_step[stream]]))
     out_ref[0] = (result[0] / result[1]).reshape(heads, tokens, width).astype(jnp.bfloat16)
 
-    def finish(i):
-        quarter, step = i // near, i % near
-
-        @pl.when(step <= last_step(quarter))
-        def _():
-            query_copy(quarter, step, own, 1).wait_send()
-            back_copy(quarter, step).wait_send()
-
-    every(quarters * near, finish)
+    for stream in streams:
+        for step in range(first_step[stream], last_step[stream] + 1):
+            query_copy(stream, step, own).wait_send()
+            back_copy(stream, step).wait_send()
     for k in range(1, groups):
         fresh_copy(k).wait_send()
 
@@ -345,18 +336,18 @@
         pltpu.VMEM((slots // TILE, 4 * rows, TILE), jnp.float32),
         pltpu.VMEM((4 * rows, LANES), jnp.float32),
         pltpu.VMEM((4 * rows, LANES), jnp.float32),
-        pltpu.VMEM((near, 4 * rows, width), jnp.bfloat16),
-        pltpu.VMEM((near, 4 * rows, 2 * width), jnp.float32),
-        pltpu.VMEM((near, 4 * rows, LANES), jnp.float32),
-        pltpu.VMEM((4, near, packed, width), jnp.bfloat16),
-        pltpu.VMEM((4, near, packed, width), jnp.bfloat16),
+        pltpu.VMEM((near + 1, 4 * rows, width), jnp.bfloat16),
+        pltpu.VMEM((near + 1, 4 * rows, 2 * width), jnp.float32),
+        pltpu.VMEM((near + 1, 4 * rows, LANES), jnp.float32),
+        pltpu.VMEM((4, near + 1, packed, width), jnp.bfloat16),
+        pltpu.VMEM((4, near + 1, packed, width), jnp.bfloat16),
         dma((7,)),
         dma((groups,)),
         dma((groups,)),
-        dma((4, near)),
-        dma((4, near)),
-        dma((4, near)),
-        dma((4, near)),
+        dma((4, near + 1)),
+        dma((4, near + 1)),
+        dma((4, near + 1)),
+        dma((4, near + 1)),
     ]
     return pl.pallas_call(
         functools.partial(kernel, levels, groups),

time: 54 us -> 49.9 us (0.924)
  the two profiles are of different devices: /device:TPU:6 before, /device:TPU:24 now
where the time goes in v9:
time: 49.9 us; the launch traced here: 49.6 us
  Pallas kernels  47.6 us (95%)
  local copies, waits for them, and re-layouts  1.35 us (3%)
  between operations  0.66 us (1%)
    pallas_call x1, Pallas kernels, per_device(): pl.pallas_call(functools.partial(kernel, levels, groups), out_shape=jax.S...  47.6 us
    unnamed x1, local copies, waits for them, and re-layouts  1.35 us

profile of v9, /device:TPU:24, one launch (start us, length us, event | category | flops | bytes accessed | tf_op | source)
XLA Modules:
  0.0 49.6 jit_solution(879773818379074974)
XLA Ops:
  0.7 47.6 %ring_attention.1 = bf16[1,4,24,128]{3,2,1,0:T(8,128)(2,1)} custom-call(bf16[1,4,24,128]{3,2,1,0:T(8,128)(2,1)} %q_hbm.1, bf16[1,4096,128]{2,1,0:T(8,128)(2,1)} %k_hbm.1, bf16[1,4096,128]{2,1,0:T(8,128)(2,1)} %v_hbm.1, s32[1]{0:T(128)S(6)} %copy.9.count_hbm, bf16[1,6,128]{2,1,0:T(8,128)(2,1)} %nk_hbm.1, bf16[1,6,128]{2,1,0:T(8,128)(2,1)} %nv_hbm.1, s32[384]{0:T(512)} %pos_hbm.1), custom_call_target="tpu_custom_call" | custom-call | flops 3221225472 | bytes 2097152 | tf_op jit(solution)/shard_map/ring_attention/pallas_call | solution.py:352
  48.2 1.3 %copy.10 = bf16[1,4,24,128]{3,2,1,0:T(8,128)(2,1)} copy(bf16[1,4,24,128]{3,2,1,0:T(8,128)(2,1)} %ring_attention.1) | data formatting | bytes 49152

commit v10 on v9

--- a/solution.py
+++ b/solution.py
@@ -8,7 +8,7 @@
 from jax.sharding import PartitionSpec as P
 
 LOG2E = 1.4426950408889634
-TILE = 1024
+TILE = 2048
 LANES = 128
 STATS = 16
 
@@ -133,11 +133,18 @@
             row = jnp.where(lane == g * STATS + i, place, row)
     place_row[...] = row
 
+    def forward(step):
+        for stream in members[step]:
+            if stream in streams:
+                query_copy(stream, step, own).wait_recv()
+                if step < last_step[stream]:
+                    query_copy(stream, step + 1, queries.at[step, part(stream, step)]).start()
+
     count = count_ref[0]
     loads[5].wait()
     loads[6].wait()
     first_key = loaded[0:16, :].astype(jnp.float32)[0:1, :]
-    chunk = 1024
+    chunk = 1024 if slots % 2048 == 0 else 512
 
     def prepare(j, _):
         base = pl.multiple_of(j * chunk, chunk)
@@ -147,10 +154,12 @@
         values[at, width:2 * width] = mass
         values[at, 0:width] = values[at, 0:width] * mass
         chosen = jnp.where(valid, loaded[at, :].astype(jnp.float32), first_key)
-        keys[:, at] = chosen.T.astype(jnp.bfloat16)
+        keys[:, at] = chosen.astype(jnp.bfloat16).T
         return 0
 
-    lax.fori_loop(0, slots // chunk, prepare, 0)
+    lax.fori_loop(0, slots // chunk // 2, prepare, 0)
+    forward(0)
+    lax.fori_loop(slots // chunk // 2, slots // chunk, prepare, 0)
 
     fresh_keys[...] = jnp.zeros_like(fresh_keys)
     fresh_values[:, 0:width] = jnp.zeros((LANES, width), jnp.bfloat16)
@@ -264,14 +273,6 @@
     def every(count, body):
         lax.fori_loop(0, count, lambda i, _: (body(i), 0)[1], 0)
 
-    def forward(step):
-        for stream in members[step]:
-            if stream in streams:
-                query_copy(stream, step, own).wait_recv()
-                if step < last_step[stream]:
-                    query_copy(stream, step + 1, queries.at[step, part(stream, step)]).start()
-
-    forward(0)
     score_start()
     every(tiles, lambda j: score_tile(0, j))
     score_end(0)

time: 49.9 us -> 49.7 us (level)
  Pallas kernels: 47.6 us -> 47 us
    pallas_call x1, Pallas kernels: 47.6 us -> 47 us  [per_device(): pl.pallas_call(functools.partial(kernel, levels, groups), out_shape=jax.S...]
where the time goes in v10:
time: 49.7 us; the launch traced here: 49 us
  Pallas kernels  47 us (95%)
  local copies, waits for them, and re-layouts  1.35 us (3%)
  between operations  0.66 us (1%)
    pallas_call x1, Pallas kernels, per_device(): pl.pallas_call(functools.partial(kernel, levels, groups), out_shape=jax.S...  47 us
    unnamed x1, local copies, waits for them, and re-layouts  1.35 us

profile of v10, /device:TPU:24, one launch (start us, length us, event | category | flops | bytes accessed | tf_op | source)
XLA Modules:
  0.0 49.0 jit_solution(11771530324247802595)
XLA Ops:
  0.7 47.0 %ring_attention.1 = bf16[1,4,24,128]{3,2,1,0:T(8,128)(2,1)} custom-call(bf16[1,4,24,128]{3,2,1,0:T(8,128)(2,1)} %q_hbm.1, bf16[1,4096,128]{2,1,0:T(8,128)(2,1)} %k_hbm.1, bf16[1,4096,128]{2,1,0:T(8,128)(2,1)} %v_hbm.1, s32[1]{0:T(128)S(6)} %copy.9.count_hbm, bf16[1,6,128]{2,1,0:T(8,128)(2,1)} %nk_hbm.1, bf16[1,6,128]{2,1,0:T(8,128)(2,1)} %nv_hbm.1, s32[384]{0:T(512)} %pos_hbm.1), custom_call_target="tpu_custom_call" | custom-call | flops 3221225472 | bytes 2097152 | tf_op jit(solution)/shard_map/ring_attention/pallas_call | solution.py:353
  47.7 1.3 %copy.10 = bf16[1,4,24,128]{3,2,1,0:T(8,128)(2,1)} copy(bf16[1,4,24,128]{3,2,1,0:T(8,128)(2,1)} %ring_attention.1) | data formatting | bytes 49152

commit v11 on v10

--- a/solution.py
+++ b/solution.py
@@ -276,10 +276,10 @@
     score_start()
     every(tiles, lambda j: score_tile(0, j))
     score_end(0)
+    forward(1)
     for step in range(steps):
         weigh_start(step)
         if step < steps - 1:
-            forward(step + 1)
             score_start()
 
             def both(j):
@@ -288,6 +288,8 @@
 
             every(tiles, both)
             score_end(step + 1)
+            if step < steps - 2:
+                forward(step + 2)
         else:
             every(tiles, lambda j: weigh_tile(step, j))
         for stream in reversed(members[step]):

time: 49.7 us -> 50.5 us (1.016)
  Pallas kernels: 47 us -> 47.6 us
    pallas_call x1, Pallas kernels: 47 us -> 47.6 us  [per_device(): pl.pallas_call(functools.partial(kernel, levels, groups), out_shape=jax.S...]
where the time goes in v11:
time: 50.5 us; the launch traced here: 49.6 us
  Pallas kernels  47.6 us (94%)
  local copies, waits for them, and re-layouts  1.35 us (3%)
  between operations  0.66 us (1%)
    pallas_call x1, Pallas kernels, per_device(): pl.pallas_call(functools.partial(kernel, levels, groups), out_shape=jax.S...  47.6 us
    unnamed x1, local copies, waits for them, and re-layouts  1.35 us

profile of v11, /device:TPU:24, one launch (start us, length us, event | category | flops | bytes accessed | tf_op | source)
XLA Modules:
  0.0 49.6 jit_solution(11786791676488555736)
XLA Ops:
  0.7 47.6 %ring_attention.1 = bf16[1,4,24,128]{3,2,1,0:T(8,128)(2,1)} custom-call(bf16[1,4,24,128]{3,2,1,0:T(8,128)(2,1)} %q_hbm.1, bf16[1,4096,128]{2,1,0:T(8,128)(2,1)} %k_hbm.1, bf16[1,4096,128]{2,1,0:T(8,128)(2,1)} %v_hbm.1, s32[1]{0:T(128)S(6)} %copy.9.count_hbm, bf16[1,6,128]{2,1,0:T(8,128)(2,1)} %nk_hbm.1, bf16[1,6,128]{2,1,0:T(8,128)(2,1)} %nv_hbm.1, s32[384]{0:T(512)} %pos_hbm.1), custom_call_target="tpu_custom_call" | custom-call | flops 3221225472 | bytes 2097152 | tf_op jit(solution)/shard_map/ring_attention/pallas_call | solution.py:355
  48.2 1.3 %copy.10 = bf16[1,4,24,128]{3,2,1,0:T(8,128)(2,1)} copy(bf16[1,4,24,128]{3,2,1,0:T(8,128)(2,1)} %ring_attention.1) | data formatting | bytes 49152
